TPU v7x, 32 devices: a whole 2x2x4 slice. The times are simulated.
32 devices in a mesh: seq: 32 (over z, y, x, core).
Axes of the slice: x: 2, y: 2, z: 4, core: 2. Of those that a mesh axis runs over, the one named last changes fastest.
Arguments:
- tokens: bfloat16 [8192, 1024], P('seq'), may hold values from -6 to 6
- w_in: bfloat16 [1024, 4096], replicated, may hold values from -0.1875 to 0.1875
- w_out: bfloat16 [1024, 1024], replicated, may hold values from -0.1875 to 0.1875
- block_counts: int32 [16], replicated, may hold values from 1 to 16, 64 in all
- tails: int32 [16], replicated, may hold values from 1 to 128
- grad_out: bfloat16 [8192, 1024], P('seq'), may hold values from -6 to 6
Outputs:
- layer_out: bfloat16 [8192, 1024], P('seq')
- grad_tokens: bfloat16 [8192, 1024], P('seq')
- grad_w_in: float32 [4096, 1024], P('seq')
Inputs may be any that keep to these rules, and one draw needn't show every extreme that they name: `block_counts`: the block counts sum to 64; one user has exactly 16 blocks.
All inputs are finite; a program needn't handle non-finite values.
Results may differ from a plain program's by a relative error of at most 0.013.
Values may be sent and summed in bfloat16 or wider, within the bound.
No kernel may reach another device: no remote copies, remote signals or barrier semaphores. Data moves between devices by JAX's collectives and lax.ppermute only.
A program may use at most 192 MiB of HBM per device.

v0:
```python
import functools

import jax
import jax.numpy as jnp
from jax import lax
from jax.experimental import pallas as pl
from jax.experimental.pallas import tpu as pltpu
from jax.sharding import Mesh, PartitionSpec as P

HEADS = 8
HD = 128
BLK = 128
MAXB = 16
SPAN = MAXB * BLK
TILE = 256
TILES = SPAN // TILE
CHUNK = 512
CHUNKS = SPAN // CHUNK
SCALE = HD ** (-0.5)
LOG2E = 1.4426950408889634

eps = 1e-05

NT = (((1,), (1,)), ((), ()))
F32, BF16 = jnp.float32, jnp.bfloat16

U, Q, V, K = (slice(i * HD, (i + 1) * HD) for i in range(4))
PLACE = (0, 2, 1, 3)
UQ, VK = slice(0, 2 * HD), slice(2 * HD, 4 * HD)


def start_kernel(counts_ref, tails_ref, w_ref, lo_ref, nv_ref, at_ref, wh_ref, sems):
    group = lax.axis_index("g").astype(jnp.int32)
    at_ref[0] = group
    head = lax.axis_index("h").astype(jnp.int32)
    at_ref[1] = head
    copies = []
    for i in range(4):
        source = w_ref.at[:, lanes_at(PLACE[i] * (w_ref.shape[0] // HD) + head)]
        copies.append(pltpu.make_async_copy(source, wh_ref.at[:, i * HD : (i + 1) * HD], sems.at[i]))
        copies[i].start()
    base = group * MAXB
    for j in range(2 * MAXB):
        lo_ref[j] = j * BLK
        nv_ref[j] = BLK

    def user(n, start):
        end = start + counts_ref[n]

        def block(j, carry):
            lo_ref[j] = (start - base) * BLK
            nv_ref[j] = jnp.where(j == end - 1 - base, tails_ref[n], BLK)
            return carry

        lax.fori_loop(jnp.maximum(start - base, 0), jnp.minimum(end - base, 2 * MAXB), block, 0)
        return end

    lax.fori_loop(0, counts_ref.shape[0], user, jnp.int32(0))
    for copy in copies:
        copy.wait()


def by_half(t, ref, shape, dim):
    side = lax.broadcasted_iota(jnp.int32, shape, dim)
    return jnp.where(side < BLK, ref[2 * t], ref[2 * t + 1])


def from_start(t, lo_ref, at, keys, dim):
    parts = [part >= lo_ref[2 * t + i] - at for i, part in enumerate(jnp.split(keys, 2, axis=1 - dim))]
    return jnp.concatenate(parts, axis=1 - dim)


def valid_rows(t, nv_ref):
    row = lax.broadcasted_iota(jnp.int32, (TILE, 1), 0)
    return (row & (BLK - 1)) < by_half(t, nv_ref, (TILE, 1), 0)


def rows_at(t):
    return pl.ds(pl.multiple_of(t * TILE, TILE), TILE)


def chunk_at(c):
    return pl.ds(pl.multiple_of(c * CHUNK, CHUNK), CHUNK)


def tiles_back(t, first, step, carry):
    count = t - first + 1

    def pair(i, carry):
        return step(pl.multiple_of((t - 2 * i - 1) * TILE, TILE), 2 * TILE, carry)

    carry = lax.fori_loop(0, count // 2, pair, carry)
    return lax.fori_loop(0, count % 2, lambda i, c: step(pl.multiple_of(first * TILE, TILE), TILE, c), carry)


def lanes_at(i):
    return pl.ds(pl.multiple_of(i * HD, HD), HD)


def norm_rows(x):
    return x * lax.rsqrt(jnp.mean(x * x, axis=-1, keepdims=True) + eps)


def silu_and_slope(pre):
    s = 0.5 + 0.5 * jnp.tanh(0.5 * pre)
    return (pre * s).astype(BF16), (s * (1.0 + pre * (1.0 - s))).astype(BF16)


def store_rows(x, place, wh_ref, normed_ref, act_ref, slope_ref, kv_ref, i):
    rows = rows_at(place)
    xn = norm_rows(x.astype(F32)).astype(BF16)
    normed_ref[rows, :] = xn
    act, slope = silu_and_slope(jnp.dot(xn, wh_ref[...], preferred_element_type=F32))
    act_ref[rows, :] = act
    slope_ref[rows, :] = slope
    kv_ref[i * TILE : (i + 1) * TILE, :] = act[:, VK]


def proj_kernel(masks, pieces, last, ahead, at_ref, *refs):
    x_refs, wh_ref = refs[: sum(pieces)], refs[sum(pieces)]
    outs = refs[-5:-1] if last else refs[-4:]
    if ahead:
        outs[3][: ahead * TILE, :] = refs[sum(pieces) + 1][...]
    for i, mask in enumerate(masks):
        parts = [ref[...] for ref in x_refs[sum(pieces[:i]) : sum(pieces[: i + 1])]]
        x = parts[0] if len(parts) == 1 else jnp.concatenate(parts, axis=0)
        store_rows(x, at_ref[1] ^ mask, wh_ref, *outs, ahead + i)
    if last:
        refs[-1][...] = outs[1][:, Q]


def proj_outs(width, n):
    return [((SPAN, width), BF16), ((SPAN, 4 * HD), BF16), ((SPAN, 4 * HD), BF16), ((n * TILE, 2 * HD), BF16)]


def project(info, masks, chunks, w, kept, last=False, kv=None):
    pieces = tuple(len(chunk) for chunk in chunks)
    flat = [piece for chunk in chunks for piece in chunk]
    lead = () if kv is None else (kv,)
    ahead = 0 if kv is None else kv.shape[0] // TILE
    start = 2 + len(flat) + len(lead)
    return call(
        functools.partial(proj_kernel, masks, pieces, last, ahead),
        (info[2],),
        (*flat, w, *lead),
        proj_outs(w.shape[0], ahead + len(masks)) + ([((SPAN, HD), BF16)] if last else []),
        after=kept,
        aliases={start + i: i for i in range(len(kept))},
    )


def cut_kernel(x_ref, y_ref, *refs):
    x_half, y_half = refs[-2:]
    x_half[...] = x_ref[:BLK, :]
    y_half[...] = y_ref[BLK:, :]


def gate_kernel(*refs):
    pass


def merge_kernel(other_ref, *refs):
    for i, ref in enumerate(refs[-3:]):
        ref[TILE:, :] = other_ref[(i + 1) * TILE : (i + 2) * TILE, :]


def places(refs):
    mine, other, *pairs = refs
    return [(mine, 0), (other, 0)] + [(ref, at) for ref in pairs for at in (0, TILE)]


def outgoing(refs):
    mine, other, *pairs = refs
    found = [(mine, 0)] * HEADS
    for i in range(4):
        found[2 * i + 1] = other, i * TILE
    for i in range(3):
        found[2 * i + 2] = pairs[i], 0
    return found


def trade_outs(cols):
    return [((TILE, cols), BF16), ((4 * TILE, cols), BF16)] + [((2 * TILE, cols), BF16)] * 3


def d_gated_kernel(at_ref, g_ref, w_ref, *refs):
    pieces, d_ref = refs[-6:-1], refs[-1]
    d_ref[...] = lax.dot_general(g_ref[...], w_ref[...], NT, preferred_element_type=F32).astype(BF16)
    for mask, (ref, at) in enumerate(outgoing(pieces)):
        ref[at : at + TILE, :] = d_ref[:, lanes_at(at_ref[1] ^ mask)]


def sigmoid(s):
    return pl.reciprocal(1.0 + jnp.exp2(s * (-SCALE * LOG2E)), approx=True)


def weigh(q, kt, v, mask):
    s = jnp.dot(q, kt, preferred_element_type=F32)
    w = jnp.where(mask, s * sigmoid(s), 0.0).astype(BF16)
    return jnp.dot(w, v, preferred_element_type=F32)


def fwd_own_kernel(lo_ref, nv_ref, act_ref, slope_ref, out_ref, kt_ref, qt_ref, slope_qt_ref):
    for t in range(TILES):
        rows = slice(t * TILE, (t + 1) * TILE)
        kt_ref[:, rows] = act_ref[rows, K].T
    row = lax.broadcasted_iota(jnp.int32, (TILE, CHUNK), 0)
    col = lax.broadcasted_iota(jnp.int32, (TILE, CHUNK), 1)

    def q_tile(t, carry):
        q = act_ref[rows_at(t), Q]

        def keys(at, size, acc):
            mask = from_start(t, lo_ref, at, col[:, :size], 1) & ((col - row)[:, :size] <= t * TILE - at)
            return acc + weigh(q, kt_ref[:, pl.ds(at, size)], act_ref[pl.ds(at, size), V], mask)

        first = jnp.maximum(lo_ref[2 * t], 0) // TILE
        acc = tiles_back(t, first, keys, jnp.zeros((TILE, HD), F32))
        out_ref[rows_at(t), :] = jnp.where(valid_rows(t, nv_ref), acc, 0.0)
        return carry

    lax.fori_loop(0, TILES, q_tile, 0)
    for t in range(TILES):
        rows = slice(t * TILE, (t + 1) * TILE)
        qt_ref[:, rows] = act_ref[rows, Q].T
        slope_qt_ref[:, rows] = slope_ref[rows, Q].T


def fwd_far_kernel(
    lo_ref, nv_ref, at_ref, act_ref, kva_ref, kvb_ref, near_ref, *refs,
):
    dg_refs, (out_ref, kv_ref, kt_ref, sum_ref, attn_s, dg_s) = refs[:5], refs[5:]
    head = at_ref[1]
    slot = 0
    for ref in (kva_ref, kvb_ref):
        for at in range(0, ref.shape[0], TILE):
            kv_ref[rows_at(slot ^ head), :] = ref[at : at + TILE, :]
            slot += 1
    for mask, (ref, at) in enumerate(places(dg_refs)):
        dg_s[rows_at(head ^ mask), :] = ref[at : at + TILE, :]
    first = jnp.minimum(lo_ref[0] + SPAN, SPAN) // CHUNK
    for t in range(TILES):
        rows = slice(t * TILE, (t + 1) * TILE)

        @pl.when(t // 2 >= first)
        def _():
            kt_ref[:, rows] = kv_ref[rows, HD:].T

    attn_s[...] = near_ref[...]
    col = lax.broadcasted_iota(jnp.int32, (TILE, CHUNK), 1)

    def q_tile(t, carry):
        q = act_ref[rows_at(t), Q]

        def k_chunk(c, acc):
            mask = from_start(t, lo_ref, c * CHUNK - SPAN, col, 1)
            return acc + weigh(q, kt_ref[:, chunk_at(c)], kv_ref[chunk_at(c), :HD], mask)

        start = (lo_ref[2 * t] + SPAN) // CHUNK
        acc = lax.fori_loop(start, CHUNKS, k_chunk, jnp.zeros((TILE, HD), F32))
        attn_s[rows_at(t), :] += jnp.where(valid_rows(t, nv_ref), acc, 0.0)
        return carry

    lax.fori_loop(0, far_tiles(lo_ref), q_tile, 0)
    ones = jnp.ones((8, HD), BF16)
    for t in range(TILES):
        rows = slice(t * TILE, (t + 1) * TILE)
        attn = attn_s[rows, :] * (SCALE / SPAN)
        out_ref[rows, :] = attn.astype(BF16)
        d_n = dg_s[rows, :].astype(F32) * act_ref[rows, U].astype(F32)
        square = lax.dot_general(ones, (attn * attn).astype(BF16), NT, preferred_element_type=F32)
        cross = lax.dot_general(ones, (attn * d_n).astype(BF16), NT, preferred_element_type=F32)
        sum_ref[t : t + 1, :] = square[:1]
        sum_ref[TILES + t : TILES + t + 1, :] = cross[:1]


def add_kernel(a_ref, b_ref, out_ref):
    out_ref[...] = (a_ref[...].astype(F32) + b_ref[...].astype(F32)).astype(out_ref.dtype)


def far_tiles(lo_ref):
    return sum((lo_ref[2 * t] < 0).astype(jnp.int32) for t in range(TILES))


def row_scales(sum_refs):
    width = HEADS * HD
    total = sum_refs[0][...]
    for ref in sum_refs[1:]:
        total += ref[...]
    r = lax.rsqrt(total[:TILES] * (1.0 / width) + eps)
    c = total[TILES:] * (1.0 / width) * r
    return jnp.concatenate([r, c], axis=0).T


def cotangent(t, scales, nv_ref, u, attn, d_gated):
    r, c = scales[:, t : t + 1], scales[:, TILES + t : TILES + t + 1]
    n = attn.astype(F32) * r
    g = r * (d_gated * u.astype(F32) - n * c)
    return n, jnp.where(valid_rows(t, nv_ref), g, 0.0).astype(BF16)


def back_scores(qt, k, v, gt, mask):
    s = jnp.dot(k, qt, preferred_element_type=F32)
    sig = jnp.where(mask, sigmoid(s), 0.0)
    dw = jnp.dot(v, gt, preferred_element_type=F32)
    ds = dw * sig * (1.0 + (s * SCALE) * (1.0 - sig))
    return (s * sig).astype(BF16), ds.astype(BF16)


def cotangent_kernel(nv_ref, at_ref, act_ref, slope_ref, attn_ref, *refs):
    sum_refs, dg_refs, (g_ref, cols_ref, dg_s) = refs[:4], refs[4:9], refs[-3:]
    for mask, (ref, at) in enumerate(places(dg_refs)):
        dg_s[rows_at(at_ref[1] ^ mask), :] = ref[at : at + TILE, :]
    scales = row_scales(sum_refs)
    for t in range(TILES):
        rows = slice(t * TILE, (t + 1) * TILE)
        d_gated = dg_s[rows, :].astype(F32)
        n, g = cotangent(t, scales, nv_ref, act_ref[rows, U], attn_ref[rows, :], d_gated)
        g_ref[rows, :] = g
        du = (d_gated * n).astype(BF16).astype(F32)
        cols_ref[:, rows] = (du * slope_ref[rows, U].astype(F32)).astype(BF16).T


def queries_kernel(lo_ref, act_ref, slope_qt_ref, qt_ref, kt_ref, g_ref, kv_ref, far_kt_ref, cols_ref, rows_ref, dkv_ref, gt_s):
    for t in range(TILES):
        rows = slice(t * TILE, (t + 1) * TILE)
        gt_s[:, rows] = g_ref[rows, :].T
    for c in range(CHUNKS):
        dkv_ref[c * CHUNK : (c + 1) * CHUNK, :] = jnp.zeros((CHUNK, 2 * HD), F32)
    key = lax.broadcasted_iota(jnp.int32, (CHUNK, TILE), 0)
    query = lax.broadcasted_iota(jnp.int32, (CHUNK, TILE), 1)

    def q_tile(t, carry):
        q, qt = act_ref[rows_at(t), Q], qt_ref[:, rows_at(t)]
        g, gt = g_ref[rows_at(t), :], gt_s[:, rows_at(t)]

        def far_chunk(c, dqt):
            at = chunk_at(c)
            mask = from_start(t, lo_ref, c * CHUNK - SPAN, key, 0)
            ds = back_scores(qt, kv_ref[at, HD:], kv_ref[at, :HD], gt, mask)[1]
            return dqt + jnp.dot(far_kt_ref[:, at], ds, preferred_element_type=F32)

        def keys(start, size, dqt):
            at = pl.ds(start, size)
            mask = from_start(t, lo_ref, start, key[:size], 0) & ((key - query)[:size] <= t * TILE - start)
            w, ds = back_scores(qt, act_ref[at, K], act_ref[at, V], gt, mask)
            dkv_ref[at, :HD] += jnp.dot(w, g, preferred_element_type=F32)
            dkv_ref[at, HD:] += jnp.dot(ds, q, preferred_element_type=F32)
            return dqt + jnp.dot(kt_ref[:, at], ds, preferred_element_type=F32)

        first = lo_ref[2 * t]
        start = jnp.minimum(first + SPAN, SPAN) // CHUNK
        dqt = lax.fori_loop(start, CHUNKS, far_chunk, jnp.zeros((HD, TILE), F32))
        dqt = tiles_back(t, jnp.maximum(first, 0) // TILE, keys, dqt)
        dq = (dqt * (SCALE / SPAN)).astype(BF16).astype(F32)
        dq = (dq * slope_qt_ref[:, rows_at(t)].astype(F32)).astype(BF16)
        cols_ref[:, rows_at(t)] = dq
        rows_ref[rows_at(t), :] = dq.T
        return carry

    lax.fori_loop(0, TILES, q_tile, 0)


def keys_kernel(
    groups, lo_ref, at_ref, own_ref, act_ref, slope_ref, q_ref, g_ref, u_cols_ref, q_cols_ref, dq_ref, attn_ref, normed_ref, *refs
):
    pieces, shares, (cols_s, all_s, acc_s) = refs[:5], refs[5:-3], refs[-3:]
    first = jnp.minimum(lo_ref[2 * TILES], SPAN) // CHUNK
    key = lax.broadcasted_iota(jnp.int32, (CHUNK, TILE), 0)

    def clear(c, carry):
        acc_s[chunk_at(c), :] = jnp.zeros((CHUNK, 2 * HD), F32)
        return carry

    lax.fori_loop(first, CHUNKS, clear, 0)

    def q_tile(t, carry):
        q, g = q_ref[rows_at(t), :], g_ref[rows_at(t), :]
        qt, gt = q.T, g.T

        def k_chunk(c, carry):
            at = chunk_at(c)
            mask = from_start(TILES + t, lo_ref, c * CHUNK, key, 0)
            w, ds = back_scores(qt, act_ref[at, K], act_ref[at, V], gt, mask)
            acc_s[at, :HD] += jnp.dot(w, g, preferred_element_type=F32)
            acc_s[at, HD:] += jnp.dot(ds, q, preferred_element_type=F32)
            return carry

        return lax.fori_loop(lo_ref[2 * (TILES + t)] // CHUNK, CHUNKS, k_chunk, carry)

    count = sum((lo_ref[2 * (TILES + t)] < SPAN).astype(jnp.int32) for t in range(TILES))
    lax.fori_loop(0, count, q_tile, 0)
    for mask, (ref, at) in enumerate(outgoing(pieces)):
        t = at_ref[1] ^ mask
        rows = rows_at(t)
        d = own_ref[rows, :] + jnp.where(t // 2 >= first, acc_s[rows, :], 0.0)
        d = (d * (SCALE / SPAN)).astype(BF16).astype(F32)
        d = (d * slope_ref[rows, VK].astype(F32)).astype(BF16)
        ref[at : at + TILE, :HD] = attn_ref[rows, :]
        ref[at : at + TILE, HD : 2 * HD] = dq_ref[rows, :]
        ref[at : at + TILE, 2 * HD :] = d
        cols_s[:, rows] = d.T
    share = jnp.dot(cols_s[...], normed_ref[...], preferred_element_type=F32).astype(BF16)
    all_s[HD : 2 * HD, :], all_s[3 * HD :, :] = share[:HD], share[HD:]
    all_s[:HD, :] = jnp.dot(u_cols_ref[...], normed_ref[...], preferred_element_type=F32).astype(BF16)
    all_s[2 * HD : 3 * HD, :] = jnp.dot(q_cols_ref[...], normed_ref[...], preferred_element_type=F32).astype(BF16)
    size = 4 * HD // groups
    for mask in range(groups):
        at = pl.multiple_of((at_ref[0] ^ mask) * size, size)
        part = all_s[pl.ds(at, size), :]
        if groups == 4:
            ref, half = shares[mask % 2], mask // 2 * size
            ref[half : half + size, :] = part.astype(ref.dtype)
        else:
            shares[mask][...] = part


def assemble(at_ref, refs, part, out_s):
    for mask, (ref, at) in enumerate(places(refs)):
        out_s[:, lanes_at(at_ref[1] ^ mask)] = ref[at : at + TILE, part * HD : (part + 1) * HD]


def branch_rows(at_ref, refs, w_ref, distances, row_s):
    width, total = w_ref.shape[0], 0.0
    for part, branch in ((1, 2), (2, 1), (3, 3)):
        assemble(at_ref, refs, part, row_s)
        for i in distances:
            at = ((at_ref[1] // 2) ^ i) * 2 * HD
            x = row_s[:, pl.ds(pl.multiple_of(at, 2 * HD), 2 * HD)]
            w = w_ref[:, pl.ds(pl.multiple_of(branch * width + at, 2 * HD), 2 * HD)]
            total += lax.dot_general(x, w, NT, preferred_element_type=F32)
    return total


def through(x, w_ref, branch):
    width = w_ref.shape[0]
    return lax.dot_general(x, w_ref[:, branch * width : (branch + 1) * width], NT, preferred_element_type=F32)


def branches_kernel(at_ref, *refs):
    pieces, (w_in_ref, dn_ref, row_s) = refs[:4], refs[4:]
    dn_ref[...] = branch_rows(at_ref, pieces, w_in_ref, (0, 1, 2), row_s)


def own_u_kernel(tokens_ref, w_in_ref, after_ref, u_ref, slope_ref):
    xn = norm_rows(tokens_ref[...].astype(F32)).astype(BF16)
    pre = jnp.dot(xn, w_in_ref[:, : tokens_ref.shape[1]], preferred_element_type=F32)
    u_ref[...], slope_ref[...] = silu_and_slope(pre)


def rows_kernel(at_ref, *refs):
    pieces, (dn_ref, dg_ref, u_ref, slope_ref, tokens_ref, grad_ref, w_out_ref, w_in_ref) = refs[:5], refs[5:-4]
    out_ref, dx_ref, end_ref, row_s = refs[-4:]
    end_ref[...] = jnp.zeros(end_ref.shape, F32)
    x = tokens_ref[...].astype(F32)
    assemble(at_ref, pieces, 0, row_s)
    attn_n = norm_rows(row_s[...].astype(F32))
    gated = (attn_n * u_ref[...].astype(F32)).astype(BF16)
    y = jnp.dot(gated, w_out_ref[...], preferred_element_type=F32)
    out_ref[...] = (x + y).astype(BF16)
    du = (dg_ref[...].astype(F32) * attn_n).astype(BF16).astype(F32)
    du = (du * slope_ref[...].astype(F32)).astype(BF16)
    dn = dn_ref[...] + through(du, w_in_ref, 0) + branch_rows(at_ref, pieces, w_in_ref, (3,), row_s)
    r = lax.rsqrt(jnp.mean(x * x, axis=-1, keepdims=True) + eps)
    n = x * r
    dx = r * (dn - n * jnp.mean(dn * n, axis=-1, keepdims=True))
    dx_ref[...] = (grad_ref[...].astype(F32) + dx).astype(BF16)


def half_kernel(keep_ref, got_ref, mine_ref, send_ref):
    size = mine_ref.shape[0]
    mine_ref[...] = keep_ref[:size, :] + got_ref[:size, :].astype(F32)
    send_ref[...] = (keep_ref[size:, :] + got_ref[size:, :].astype(F32)).astype(BF16)


def sum_kernel(*refs):
    total = refs[0][...].astype(F32)
    for ref in refs[1:-2]:
        total += ref[...].astype(F32)
    refs[-1][...] = total


def call(kernel, scalars, arrays, outs, scratch=(), after=(), aliases=None, limit=16, sems=0):
    smem = pl.BlockSpec(memory_space=pltpu.SMEM)
    vmem = pl.BlockSpec(memory_space=pltpu.VMEM)
    anywhere = pl.BlockSpec(memory_space=pl.ANY)
    return pl.pallas_call(
        kernel,
        out_shape=[jax.ShapeDtypeStruct(*out) for out in outs],
        in_specs=[smem] * len(scalars) + [vmem] * len(arrays) + [anywhere] * len(after),
        out_specs=[smem if out[1] == jnp.int32 else vmem for out in outs],
        scratch_shapes=[pltpu.VMEM(*shape) for shape in scratch] + ([pltpu.SemaphoreType.DMA((sems,))] if sems else []),
        input_output_aliases=aliases or {},
        compiler_params=pltpu.CompilerParams(vmem_limit_bytes=limit * 2**20),
        cost_estimate=pl.CostEstimate(flops=0, bytes_accessed=0, transcendentals=0),
    )(*scalars, *arrays, *after)


def per_device(groups, tokens, w_in, w_out, block_counts, tails, grad_out):
    count, width = tokens.shape
    own, tall, wide, tall_t = (count, width), (SPAN, HD), (SPAN, 2 * HD), (HD, SPAN)
    piece, half, sums_shape = (count, HD), (BLK, width), (2 * TILES, TILE)

    def swap(x, mask):
        return lax.ppermute(x, "h", [(i, i ^ mask) for i in range(HEADS)])

    def onward(x):
        return lax.ppermute(x, "g", [(i, i + 1) for i in range(groups - 1)])

    def backward(x):
        return lax.ppermute(x, "g", [(i + 1, i) for i in range(groups - 1)])

    def trade(pieces, after=()):
        mine, other, *pairs = pieces
        other = swap(other, 1)
        pairs = call(
            merge_kernel,
            (),
            (other,),
            [(x.shape, BF16) for x in pairs],
            after=(*pairs, *after),
            aliases={1: 0, 2: 1, 3: 2},
            limit=4,
        )
        return [mine, other] + [swap(x, mask) for x, mask in zip(pairs, (2, 4, 6))]

    x_rows, y_rows = swap(tokens, 2), swap(tokens, 4)
    other = swap(tokens, 1)
    *info, w_head = call(
        start_kernel,
        (block_counts, tails),
        (),
        [((2 * MAXB,), jnp.int32)] * 2 + [((2,), jnp.int32), ((width, 4 * HD), BF16)],
        after=(w_in,),
        limit=51,
        sems=4,
    )
    *kept, kv = project(info, (0, 1), ((tokens,), (other,)), w_head, ())
    *dg_pieces, dg_own = call(
        d_gated_kernel, info[2:], (grad_out, w_out), trade_outs(HD) + [(own, BF16)], after=(kv,)
    )
    x_rows, y_rows, x_half, y_half = call(
        cut_kernel,
        (),
        (x_rows, y_rows),
        [(own, BF16), (own, BF16), (half, BF16), (half, BF16)],
        after=(kv, dg_own),
        aliases={0: 0, 1: 1},
        limit=4,
    )
    corner = swap(x_half, 4), swap(y_half, 2)
    chunks = ((x_rows,), (swap(x_rows, 1),), (y_rows,), (swap(y_rows, 1),))
    *kept, kv = project(info, (2, 3, 4, 5), chunks, w_head, kept, kv=kv)
    far_kv = [onward(kv)]
    corner = call(gate_kernel, (), (), [(half, BF16), (half, BF16)], after=(*corner, kv), aliases={0: 0, 1: 1}, limit=4)
    *kept, kv, q = project(info, (6, 7), (corner, [swap(x, 1) for x in corner]), w_head, kept, True)
    far_kv.append(onward(kv))
    q_next = backward(q)
    normed, act, slope = kept
    d_gated = trade(dg_pieces, (kv,))

    near, kt, qt, slope_qt = call(fwd_own_kernel, info[:2], (act, slope), [(tall, F32)] + [(tall_t, BF16)] * 3)
    attn, kv, far_kt, sums = call(
        fwd_far_kernel,
        info,
        (act, *far_kv, near, *d_gated),
        [(tall, BF16), (wide, BF16), (tall_t, BF16), (sums_shape, F32)],
        [(tall, F32), (tall, BF16)],
    )
    sums = call(add_kernel, (), (sums, swap(sums, 1)), [(sums_shape, F32)], limit=4)[0]
    sums = [sums] + [swap(sums, mask) for mask in (2, 4, 6)]

    g, u_cols = call(
        cotangent_kernel,
        info[1:],
        (act, slope, attn, *sums, *d_gated),
        [(tall, BF16), (tall_t, BF16)],
        [(tall, BF16)],
        (q_next,),
    )
    g_next = backward(g)
    q_cols, d_q, dkv = call(
        queries_kernel,
        info[:1],
        (act, slope_qt, qt, kt, g, kv, far_kt),
        [(tall_t, BF16), (tall, BF16), (wide, F32)],
        [(tall_t, BF16)],
    )
    rows, cols = 4 * HD // groups, 4 * HD
    outs = call(
        functools.partial(keys_kernel, groups),
        (info[0], info[2]),
        (dkv, act, slope, q_next, g_next, u_cols, q_cols, d_q, attn, normed),
        trade_outs(cols)
        + ([((2 * rows, width), F32), ((2 * rows, width), BF16)] if groups == 4 else [((rows, width), BF16)] * groups),
        [((2 * HD, SPAN), BF16), ((4 * HD, width), BF16), (wide, F32)],
    )
    def between(x, mask):
        return lax.ppermute(x, "g", [(i, i ^ mask) for i in range(groups)])

    if groups == 4:
        keep, send = outs[5:]
        half = [((rows, width), F32), ((rows, width), BF16)]
        keep, send = call(half_kernel, (), (keep, between(send, 1)), half, limit=8)
        shares = keep, between(send, 2)
    else:
        shares = [outs[5]] + [between(x, mask + 1) for mask, x in enumerate(outs[6:])]
    pieces = trade(outs[:5])
    u, slope_u = call(own_u_kernel, (), (tokens, w_in), [(own, BF16), (own, BF16)], after=(outs[0],))
    d_normed = call(
        branches_kernel,
        info[2:],
        (*pieces[:4], w_in),
        [(own, F32)],
        [(own, BF16)],
    )[0]
    layer_out, grad_tokens, end = call(
        rows_kernel,
        info[2:],
        (*pieces, d_normed, dg_own, u, slope_u, tokens, grad_out, w_out, w_in),
        [(own, BF16), (own, BF16), ((8, HD), F32)],
        [(own, BF16)],
    )
    grad_w_in = call(
        sum_kernel, (), tuple(shares), [((rows, width), F32)], after=(end,)
    )[0]
    parts = groups // 4
    if parts > 1:
        perm = [
            (i * HEADS + j, ((i // parts) * HEADS + j) * parts + i % parts)
            for i in range(groups)
            for j in range(HEADS)
        ]
        grad_w_in = lax.ppermute(grad_w_in, ("g", "h"), perm)
    return (layer_out, grad_tokens, grad_w_in)


def solution(mesh):
    groups = mesh.shape["seq"] // HEADS
    split = Mesh(mesh.devices.reshape(groups, HEADS), ("g", "h"))
    rows = P(("g", "h"), None)
    return jax.shard_map(
        functools.partial(per_device, groups),
        mesh=split,
        in_specs=(rows, P(), P(), P(), P(), rows),
        out_specs=(rows, rows, rows),
        check_vma=False,
    )
```

profile of v0, /device:TPU:0, one launch (start us, length us, event | category | flops | bytes accessed | tf_op | source)
XLA Modules:
  0.0 121.7 jit_solution(5650450585596090886)
XLA Ops:
  1.2 2.6 %collective-permute-start.1 = (bf16[256,1024]{1,0:T(8,128)(2,1)}, bf16[256,1024]{1,0:T(8,128)(2,1)S(1)}, u32[]{:S(2)}, u32[]{:S(2)}) collective-permute-start(bf16[256,1024]{1,0:T(8,128)(2,1)} %refs_9_.1), channel_id=1, source_target_pairs={{0,4},{1,5},{2,6},{3,7},{4,0},{5,1},{6,2},{7,3},{8,12},{9,13},{10,... | collective-permute-start | bytes 1572872 | tf_op jit(solution)/shard_map/ppermute | solution.py:505
  3.8 1.5 %collective-permute-start = (bf16[256,1024]{1,0:T(8,128)(2,1)}, bf16[256,1024]{1,0:T(8,128)(2,1)S(1)}, u32[]{:S(2)}, u32[]{:S(2)}) collective-permute-start(bf16[256,1024]{1,0:T(8,128)(2,1)} %refs_9_.1), channel_id=1, source_target_pairs={{0,2},{1,3},{2,0},{3,1},{4,6},{5,7},{6,4},{7,5},{8,10},{9,11},{10,... | collective-permute-start | bytes 1572872 | tf_op jit(solution)/shard_map/ppermute | solution.py:505
  6.6 2.4 %shard_map.85 = (s32[32]{0:T(128)S(1)}, s32[32]{0:T(128)S(1)}, s32[2]{0:T(128)S(1)}, bf16[1024,512]{1,0:T(8,128)(2,1)S(1)}) custom-call(s32[16]{0:T(128)S(1)} %copy-done.3, s32[16]{0:T(128)S(1)} %copy-done.4, bf16[1024,4096]{1,0:T(8,128)(2,1)} %refs_12_.1), custom_call_target="tpu_custom_call" | custom-call | tf_op jit(solution)/shard_map/pallas_call | solution.py:487
  9.0 1.7 %shard_map.86 = (bf16[2048,1024]{1,0:T(8,128)(2,1)S(1)}, bf16[2048,512]{1,0:T(8,128)(2,1)S(1)}, bf16[2048,512]{1,0:T(8,128)(2,1)S(1)}, bf16[512,256]{1,0:T(8,128)(2,1)S(1)}) custom-call(s32[2]{0:T(128)S(1)} %get-tuple-element.65.at_ref, bf16[256,1024]{1,0:T(8,128)(2,1)S(1)} %copy-done.1, bf16[256,1024]{1,0:T(8,128)(2,1)S(1)} %collective-permute-done.2.refs_1_, ...), custom_call_target="tpu_custom_call" | custom-call | tf_op jit(solution)/shard_map/pallas_call | solution.py:487
  10.7 1.4 %shard_map.87 = (bf16[256,128]{1,0:T(8,128)(2,1)S(1)}, bf16[1024,128]{1,0:T(8,128)(2,1)S(1)}, bf16[512,128]{1,0:T(8,128)(2,1)S(1)}, bf16[512,128]{1,0:T(8,128)(2...) custom-call(s32[2]{0:T(128)S(1)} %get-tuple-element.65.at_ref, bf16[256,1024]{1,0:T(8,128)(2,1)S(1)} %copy-done.2, ...), custom_call_target="tpu_custom_call" | custom-call | tf_op jit(solution)/shard_map/pallas_call | solution.py:487
  12.1 4.4 %collective-permute-done.1.y_ref = bf16[256,1024]{1,0:T(8,128)(2,1)S(1)} collective-permute-done((bf16[256,1024]{1,0:T(8,128)(2,1)}, bf16[256,1024]{1,0:T(8,128)(2,1)S(1)}, u32[]{:S(2)}, u32[]{:S(2)}) %collective-permute-start.1) | collective-permute-done | bytes 524320 | tf_op jit(solution)/shard_map/ppermute | solution.py:505
  16.5 1.5 %collective-permute-done.x_ref = bf16[256,1024]{1,0:T(8,128)(2,1)S(1)} collective-permute-done((bf16[256,1024]{1,0:T(8,128)(2,1)}, bf16[256,1024]{1,0:T(8,128)(2,1)S(1)}, u32[]{:S(2)}, u32[]{:S(2)}) %collective-permute-start) | collective-permute-done | bytes 524320 | tf_op jit(solution)/shard_map/ppermute | solution.py:505
  18.9 1.7 %collective-permute-start.4 = (bf16[128,1024]{1,0:T(8,128)(2,1)S(1)}, bf16[128,1024]{1,0:T(8,128)(2,1)S(1)}, u32[]{:S(2)}, u32[]{:S(2)}) collective-permute-start(bf16[128,1024]{1,0:T(8,128)(2,1)S(1)} %get-tuple-element.71), channel_id=1, source_target_pairs={{0,2},{1,3},{2,0},{3,1},{4,6},{5,7},{6,4},{7,5},{8,10},{9,11},{10,... | collective-permute-start | bytes 786440 | tf_op jit(solution)/shard_map/ppermute | solution.py:505
  20.7 2.6 %shard_map.89 = (bf16[2048,1024]{1,0:T(8,128)(2,1)S(1)}, bf16[2048,512]{1,0:T(8,128)(2,1)S(1)}, bf16[2048,512]{1,0:T(8,128)(2,1)S(1)}, bf16[1536,256]{1,0:T(8,128)(2,1)S(1)}) custom-call(s32[2]{0:T(128)S(1)} %get-tuple-element.65.at_ref, bf16[256,1024]{1,0:T(8,128)(2,1)S(1)} %get-tuple-element.72.refs_0_, ...), custom_call_target="tpu_custom_call", output_to_operand_aliasing={{0}: (7, {}), {1}: (8, {}), {2}: (9, {})} | custom-call | tf_op jit(solution)/shard_map/pallas_call | solution.py:487
  23.3 3.5 %collective-permute-start.9 = (bf16[1536,256]{1,0:T(8,128)(2,1)S(1)}, bf16[1536,256]{1,0:T(8,128)(2,1)S(1)}, u32[]{:S(2)}, u32[]{:S(2)}) collective-permute-start(bf16[1536,256]{1,0:T(8,128)(2,1)S(1)} %get-tuple-element.77.refs_2_), channel_id=1, source_target_pairs={{0,8},{8,16},{16,24},{1,9},{9,17},{17,25},{2,10},{10,18},{18,26},{... | collective-permute-start | bytes 2359304 | tf_op jit(solution)/shard_map/ppermute | solution.py:508
  28.9 1.8 %shard_map.91 = (bf16[2048,1024]{1,0:T(8,128)(2,1)S(1)}, bf16[2048,512]{1,0:T(8,128)(2,1)S(1)}, bf16[2048,512]{1,0:T(8,128)(2,1)S(1)}, bf16[512,256]{1,0:T(8,128)(2,1)S(1)}, bf16[2048,128]{1,0:T(8,128)(2,1)S(1)}) custom-call(s32[2]{0:T(128)S(1)} %get-tuple-element.65.at_ref, ...), custom_call_target="tpu_custom_call", output_to_operand_aliasing={{0}: (6, {}), {1}: (7, {}), {2}: (8, {})} | custom-call | tf_op jit(solution)/shard_map/pallas_call | solution.py:487
  30.7 1.3 %collective-permute-start.19 = (bf16[2048,128]{1,0:T(8,128)(2,1)S(1)}, bf16[2048,128]{1,0:T(8,128)(2,1)S(1)}, u32[]{:S(2)}, u32[]{:S(2)}) collective-permute-start(bf16[2048,128]{1,0:T(8,128)(2,1)S(1)} %get-tuple-element.101), channel_id=1, source_target_pairs={{8,0},{16,8},{24,16},{9,1},{17,9},{25,17},{10,2},{18,10},{26,18},{... | collective-permute-start | bytes 1572872 | tf_op jit(solution)/shard_map/ppermute | solution.py:511
  32.0 1.7 %collective-permute-start.12 = (bf16[512,128]{1,0:T(8,128)(2,1)S(1)}, bf16[512,128]{1,0:T(8,128)(2,1)S(1)}, u32[]{:S(2)}, u32[]{:S(2)}) collective-permute-start(bf16[512,128]{1,0:T(8,128)(2,1)S(1)} %get-tuple-element.96), channel_id=1, source_target_pairs={{0,2},{1,3},{2,0},{3,1},{4,6},{5,7},{6,4},{7,5},{8,10},{9,11},{10,... | collective-permute-start | bytes 393224 | tf_op jit(solution)/shard_map/ppermute | solution.py:505
  33.7 4.5 %collective-permute-start.10 = (bf16[512,256]{1,0:T(8,128)(2,1)S(1)}, bf16[512,256]{1,0:T(8,128)(2,1)S(1)}, u32[]{:S(2)}, u32[]{:S(2)}) collective-permute-start(bf16[512,256]{1,0:T(8,128)(2,1)S(1)} %get-tuple-element.89.refs_3_), channel_id=1, source_target_pairs={{0,8},{8,16},{16,24},{1,9},{9,17},{17,25},{2,10},{10,18},{18,26},{... | collective-permute-start | bytes 786440 | tf_op jit(solution)/shard_map/ppermute | solution.py:508
  38.2 1.6 %collective-permute-start.13 = (bf16[512,128]{1,0:T(8,128)(2,1)S(1)}, bf16[512,128]{1,0:T(8,128)(2,1)S(1)}, u32[]{:S(2)}, u32[]{:S(2)}) collective-permute-start(bf16[512,128]{1,0:T(8,128)(2,1)S(1)} %get-tuple-element.97), channel_id=1, source_target_pairs={{0,4},{1,5},{2,6},{3,7},{4,0},{5,1},{6,2},{7,3},{8,12},{9,13},{10,... | collective-permute-start | bytes 393224 | tf_op jit(solution)/shard_map/ppermute | solution.py:505
  40.2 7.2 %shard_map.92 = (f32[2048,128]{1,0:T(8,128)S(1)}, bf16[128,2048]{1,0:T(8,128)(2,1)S(1)}, bf16[128,2048]{1,0:T(8,128)(2,1)S(1)}, bf16[128,2048]{1,0:T(8,128)(2,1)S(1)}) custom-call(s32[32]{0:T(128)S(1)} %get-tuple-element.66.lo_ref, s32[32]{0:T(128)S(1)} %get-tuple-element.84.nv_ref, bf16[2048,512]{1,0:T(8,128)(2,1)S(1)} %get-tuple-element.83.act_ref, ...), custom_call_target="tpu_custom_call" | custom-call | tf_op jit(solution)/shard_map/pallas_call | solution.py:487
  47.4 2.1 %collective-permute-done.10.kvb_ref = bf16[512,256]{1,0:T(8,128)(2,1)S(1)} collective-permute-done((bf16[512,256]{1,0:T(8,128)(2,1)S(1)}, bf16[512,256]{1,0:T(8,128)(2,1)S(1)}, u32[]{:S(2)}, u32[]{:S(2)}) %collective-permute-start.10) | collective-permute-done | bytes 262176 | tf_op jit(solution)/shard_map/ppermute | solution.py:508
  51.9 1.4 %collective-permute-start.18 = (f32[16,256]{1,0:T(8,128)S(1)}, f32[16,256]{1,0:T(8,128)S(1)}, u32[]{:S(2)}, u32[]{:S(2)}) collective-permute-start(f32[16,256]{1,0:T(8,128)S(1)} %shard_map.95.refs_0_), channel_id=1, source_target_pairs={{0,6},{1,7},{2,4},{3,5},{4,2},{5,3},{6,0},{7,1},{8,14},{9,15},{10,... | collective-permute-start | bytes 49160 | tf_op jit(solution)/shard_map/ppermute | solution.py:505
  53.3 1.5 %collective-permute-start.17 = (f32[16,256]{1,0:T(8,128)S(1)}, f32[16,256]{1,0:T(8,128)S(1)}, u32[]{:S(2)}, u32[]{:S(2)}) collective-permute-start(f32[16,256]{1,0:T(8,128)S(1)} %shard_map.95.refs_0_), channel_id=1, source_target_pairs={{0,4},{1,5},{2,6},{3,7},{4,0},{5,1},{6,2},{7,3},{8,12},{9,13},{10,... | collective-permute-start | bytes 49160 | tf_op jit(solution)/shard_map/ppermute | solution.py:505
  57.1 1.5 %collective-permute-done.16.refs_1_ = f32[16,256]{1,0:T(8,128)S(1)} collective-permute-done((f32[16,256]{1,0:T(8,128)S(1)}, f32[16,256]{1,0:T(8,128)S(1)}, u32[]{:S(2)}, u32[]{:S(2)}) %collective-permute-start.16) | collective-permute-done | bytes 16416 | tf_op jit(solution)/shard_map/ppermute | solution.py:505
  58.6 1.8 %shard_map.96 = (bf16[2048,128]{1,0:T(8,128)(2,1)S(1)}, bf16[128,2048]{1,0:T(8,128)(2,1)S(1)}) custom-call(s32[32]{0:T(128)S(1)} %get-tuple-element.84.nv_ref, s32[2]{0:T(128)S(1)} %get-tuple-element.65.at_ref, bf16[2048,512]{1,0:T(8,128)(2,1)S(1)} %get-tuple-element.83.act_ref, bf16[2048,512]{1,0:T(8,128)(2,1)S(1)} %get-tuple-element.85.slope_ref, ...), custom_call_target="tpu_custom_call" | custom-call | tf_op jit(solution)/shard_map/pallas_call | solution.py:487
  60.4 1.3 %collective-permute-start.20 = (bf16[2048,128]{1,0:T(8,128)(2,1)S(1)}, bf16[2048,128]{1,0:T(8,128)(2,1)S(1)}, u32[]{:S(2)}, u32[]{:S(2)}) collective-permute-start(bf16[2048,128]{1,0:T(8,128)(2,1)S(1)} %get-tuple-element.102.g_ref), channel_id=1, source_target_pairs={{8,0},{16,8},{24,16},{9,1},{17,9},{25,17},{10,2},{18,10},{26,18},{... | collective-permute-start | bytes 1572872 | tf_op jit(solution)/shard_map/ppermute | solution.py:511
  61.7 10.4 %shard_map.97 = (bf16[128,2048]{1,0:T(8,128)(2,1)S(1)}, bf16[2048,128]{1,0:T(8,128)(2,1)S(1)}, f32[2048,256]{1,0:T(8,128)S(1)}) custom-call(s32[32]{0:T(128)S(1)} %get-tuple-element.66.lo_ref, bf16[2048,512]{1,0:T(8,128)(2,1)S(1)} %get-tuple-element.83.act_ref, bf16[128,2048]{1,0:T(8,128)(2,1)S(1)} %get-tuple-element.86.slope_qt_ref, ...), custom_call_target="tpu_custom_call" | custom-call | tf_op jit(solution)/shard_map/pallas_call | solution.py:487
  72.1 6.3 %collective-permute-done.20.g_ref = bf16[2048,128]{1,0:T(8,128)(2,1)S(1)} collective-permute-done((bf16[2048,128]{1,0:T(8,128)(2,1)S(1)}, bf16[2048,128]{1,0:T(8,128)(2,1)S(1)}, u32[]{:S(2)}, u32[]{:S(2)}) %collective-permute-start.20) | collective-permute-done | bytes 524320 | tf_op jit(solution)/shard_map/ppermute | solution.py:511
  78.4 7.7 %shard_map.98 = (bf16[256,512]{1,0:T(8,128)(2,1)S(1)}, bf16[1024,512]{1,0:T(8,128)(2,1)S(1)}, bf16[512,512]{1,0:T(8,128)(2,1)S(1)}, bf16[512,512]{1,0:T(8,128)(2...) custom-call(s32[32]{0:T(128)S(1)} %get-tuple-element.66.lo_ref, ...), custom_call_target="tpu_custom_call" | custom-call | tf_op jit(solution)/shard_map/pallas_call | solution.py:487
  86.2 1.5 %collective-permute-start.25 = (bf16[256,1024]{1,0:T(8,128)(2,1)S(1)}, bf16[256,1024]{1,0:T(8,128)(2,1)S(1)}, u32[]{:S(2)}, u32[]{:S(2)}) collective-permute-start(bf16[256,1024]{1,0:T(8,128)(2,1)S(1)} %get-tuple-element.123), channel_id=1, source_target_pairs={{0,8},{8,0},{16,24},{24,16},{1,9},{9,1},{17,25},{25,17},{2,10},{10... | collective-permute-start | bytes 1572872 | tf_op jit(solution)/shard_map/ppermute | solution.py:599
  90.4 2.0 %collective-permute-start.24 = (bf16[512,512]{1,0:T(8,128)(2,1)S(1)}, bf16[512,512]{1,0:T(8,128)(2,1)S(1)}, u32[]{:S(2)}, u32[]{:S(2)}) collective-permute-start(bf16[512,512]{1,0:T(8,128)(2,1)S(1)} %get-tuple-element.117), channel_id=1, source_target_pairs={{0,6},{1,7},{2,4},{3,5},{4,2},{5,3},{6,0},{7,1},{8,14},{9,15},{10,... | collective-permute-start | bytes 1572872 | tf_op jit(solution)/shard_map/ppermute | solution.py:505
  92.5 8.1 %collective-permute-done.25.got_ref = bf16[256,1024]{1,0:T(8,128)(2,1)S(1)} collective-permute-done((bf16[256,1024]{1,0:T(8,128)(2,1)S(1)}, bf16[256,1024]{1,0:T(8,128)(2,1)S(1)}, u32[]{:S(2)}, u32[]{:S(2)}) %collective-permute-start.25) | collective-permute-done | bytes 524320 | tf_op jit(solution)/shard_map/ppermute | solution.py:599
  101.8 1.9 %collective-permute-done.22.refs_2_ = bf16[512,512]{1,0:T(8,128)(2,1)S(1)} collective-permute-done((bf16[512,512]{1,0:T(8,128)(2,1)S(1)}, bf16[512,512]{1,0:T(8,128)(2,1)S(1)}, u32[]{:S(2)}, u32[]{:S(2)}) %collective-permute-start.22) | collective-permute-done | bytes 524320 | tf_op jit(solution)/shard_map/ppermute | solution.py:505
  103.7 10.8 %collective-permute-done.23.refs_3_ = bf16[512,512]{1,0:T(8,128)(2,1)S(1)} collective-permute-done((bf16[512,512]{1,0:T(8,128)(2,1)S(1)}, bf16[512,512]{1,0:T(8,128)(2,1)S(1)}, u32[]{:S(2)}, u32[]{:S(2)}) %collective-permute-start.23) | collective-permute-done | bytes 524320 | tf_op jit(solution)/shard_map/ppermute | solution.py:505
  114.6 2.2 %shard_map.100.refs_5_ = f32[256,1024]{1,0:T(8,128)S(1)} custom-call(s32[2]{0:T(128)S(1)} %get-tuple-element.65.at_ref, bf16[256,512]{1,0:T(8,128)(2,1)S(1)} %get-tuple-element.110.refs_0_.after_ref, bf16[1024,512]{1,0:T(8,128)(2,1)S(1)} %collective-permute-done.21.other_ref.refs_1_, bf16[512,512]{1,0:T(8,128)(2,1)S(1)} %collective-permute-done.22.refs_2_, ...), custom_call_target="tpu_custom_call" | custom-call | tf_op jit(solution)/shard_map/pallas_call | solution.py:487
  116.8 4.1 %shard_map.102 = (bf16[256,1024]{1,0:T(8,128)(2,1)}, bf16[256,1024]{1,0:T(8,128)(2,1)}, f32[8,128]{1,0:T(8,128)S(1)}) custom-call(s32[2]{0:T(128)S(1)} %get-tuple-element.65.at_ref, bf16[256,512]{1,0:T(8,128)(2,1)S(1)} %get-tuple-element.110.refs_0_.after_ref, bf16[1024,512]{1,0:T(8,128)(2,1)S(1)} %collective-permute-done.21.other_ref.refs_1_, ...), custom_call_target="tpu_custom_call" | custom-call | tf_op jit(solution)/shard_map/pallas_call | solution.py:487
  (57 shorter events, 14.7 us)
Async XLA Ops:
  0.6 8.4 %copy-start.1 = (bf16[256,1024]{1,0:T(8,128)(2,1)S(1)}, bf16[256,1024]{1,0:T(8,128)(2,1)}, u32[]{:S(2)}) copy-start(bf16[256,1024]{1,0:T(8,128)(2,1)} %refs_9_.1) | copy-start | bytes 1572868
  0.6 8.3 %collective-permute-start.2 = (bf16[256,1024]{1,0:T(8,128)(2,1)}, bf16[256,1024]{1,0:T(8,128)(2,1)S(1)}, u32[]{:S(2)}, u32[]{:S(2)}) collective-permute-start(bf16[256,1024]{1,0:T(8,128)(2,1)} %refs_9_.1), channel_id=1, source_target_pairs={{0,1},{1,0},{2,3},{3,2},{4,5},{5,4},{6,7},{7,6},{8,9},{9,8},{10,11... | collective-permute-start | bytes 1572872 | tf_op jit(solution)/shard_map/ppermute | solution.py:505
  1.2 15.3 %collective-permute-start.1 = (bf16[256,1024]{1,0:T(8,128)(2,1)}, bf16[256,1024]{1,0:T(8,128)(2,1)S(1)}, u32[]{:S(2)}, u32[]{:S(2)}) collective-permute-start(bf16[256,1024]{1,0:T(8,128)(2,1)} %refs_9_.1), channel_id=1, source_target_pairs={{0,4},{1,5},{2,6},{3,7},{4,0},{5,1},{6,2},{7,3},{8,12},{9,13},{10,... | collective-permute-start | bytes 1572872 | tf_op jit(solution)/shard_map/ppermute | solution.py:505
  3.8 14.2 %collective-permute-start = (bf16[256,1024]{1,0:T(8,128)(2,1)}, bf16[256,1024]{1,0:T(8,128)(2,1)S(1)}, u32[]{:S(2)}, u32[]{:S(2)}) collective-permute-start(bf16[256,1024]{1,0:T(8,128)(2,1)} %refs_9_.1), channel_id=1, source_target_pairs={{0,2},{1,3},{2,0},{3,1},{4,6},{5,7},{6,4},{7,5},{8,10},{9,11},{10,... | collective-permute-start | bytes 1572872 | tf_op jit(solution)/shard_map/ppermute | solution.py:505
  6.6 4.1 %copy-start.2 = (bf16[256,1024]{1,0:T(8,128)(2,1)S(1)}, bf16[256,1024]{1,0:T(8,128)(2,1)}, u32[]{:S(2)}) copy-start(bf16[256,1024]{1,0:T(8,128)(2,1)} %refs_10_.1) | copy-start | bytes 1572868
  9.0 1.7 %copy-start = (bf16[1024,1024]{1,0:T(8,128)(2,1)S(1)}, bf16[1024,1024]{1,0:T(8,128)(2,1)}, u32[]{:S(2)}) copy-start(bf16[1024,1024]{1,0:T(8,128)(2,1)} %refs_11_.1) | copy-start | bytes 6291460
  18.0 2.6 %collective-permute-start.5 = (bf16[256,1024]{1,0:T(8,128)(2,1)S(1)}, bf16[256,1024]{1,0:T(8,128)(2,1)S(1)}, u32[]{:S(2)}, u32[]{:S(2)}) collective-permute-start(bf16[256,1024]{1,0:T(8,128)(2,1)S(1)} %get-tuple-element.72.refs_0_), channel_id=1, source_target_pairs={{0,1},{1,0},{2,3},{3,2},{4,5},{5,4},{6,7},{7,6},{8,9},{9,8},{10,11... | collective-permute-start | bytes 1572872 | tf_op jit(solution)/shard_map/ppermute | solution.py:505
  18.1 2.6 %collective-permute-start.6 = (bf16[256,1024]{1,0:T(8,128)(2,1)S(1)}, bf16[256,1024]{1,0:T(8,128)(2,1)S(1)}, u32[]{:S(2)}, u32[]{:S(2)}) collective-permute-start(bf16[256,1024]{1,0:T(8,128)(2,1)S(1)} %get-tuple-element.73.refs_2_), channel_id=1, source_target_pairs={{0,1},{1,0},{2,3},{3,2},{4,5},{5,4},{6,7},{7,6},{8,9},{9,8},{10,11... | collective-permute-start | bytes 1572872 | tf_op jit(solution)/shard_map/ppermute | solution.py:505
  18.6 8.3 %collective-permute-start.3 = (bf16[128,1024]{1,0:T(8,128)(2,1)S(1)}, bf16[128,1024]{1,0:T(8,128)(2,1)S(1)}, u32[]{:S(2)}, u32[]{:S(2)}) collective-permute-start(bf16[128,1024]{1,0:T(8,128)(2,1)S(1)} %get-tuple-element.70), channel_id=1, source_target_pairs={{0,4},{1,5},{2,6},{3,7},{4,0},{5,1},{6,2},{7,3},{8,12},{9,13},{10,... | collective-permute-start | bytes 786440 | tf_op jit(solution)/shard_map/ppermute | solution.py:505
  18.9 8.0 %collective-permute-start.4 = (bf16[128,1024]{1,0:T(8,128)(2,1)S(1)}, bf16[128,1024]{1,0:T(8,128)(2,1)S(1)}, u32[]{:S(2)}, u32[]{:S(2)}) collective-permute-start(bf16[128,1024]{1,0:T(8,128)(2,1)S(1)} %get-tuple-element.71), channel_id=1, source_target_pairs={{0,2},{1,3},{2,0},{3,1},{4,6},{5,7},{6,4},{7,5},{8,10},{9,11},{10,... | collective-permute-start | bytes 786440 | tf_op jit(solution)/shard_map/ppermute | solution.py:505
  23.3 26.2 %collective-permute-start.9 = (bf16[1536,256]{1,0:T(8,128)(2,1)S(1)}, bf16[1536,256]{1,0:T(8,128)(2,1)S(1)}, u32[]{:S(2)}, u32[]{:S(2)}) collective-permute-start(bf16[1536,256]{1,0:T(8,128)(2,1)S(1)} %get-tuple-element.77.refs_2_), channel_id=1, source_target_pairs={{0,8},{8,16},{16,24},{1,9},{9,17},{17,25},{2,10},{10,18},{18,26},{... | collective-permute-start | bytes 2359304 | tf_op jit(solution)/shard_map/ppermute | solution.py:508
  26.9 1.6 %collective-permute-start.7 = (bf16[128,1024]{1,0:T(8,128)(2,1)S(1)}, bf16[128,1024]{1,0:T(8,128)(2,1)S(1)}, u32[]{:S(2)}, u32[]{:S(2)}) collective-permute-start(bf16[128,1024]{1,0:T(8,128)(2,1)S(1)} %get-tuple-element.78.refs_0_), channel_id=1, source_target_pairs={{0,1},{1,0},{2,3},{3,2},{4,5},{5,4},{6,7},{7,6},{8,9},{9,8},{10,11... | collective-permute-start | bytes 786440 | tf_op jit(solution)/shard_map/ppermute | solution.py:505
  27.0 1.9 %collective-permute-start.8 = (bf16[128,1024]{1,0:T(8,128)(2,1)S(1)}, bf16[128,1024]{1,0:T(8,128)(2,1)S(1)}, u32[]{:S(2)}, u32[]{:S(2)}) collective-permute-start(bf16[128,1024]{1,0:T(8,128)(2,1)S(1)} %get-tuple-element.79.refs_1_), channel_id=1, source_target_pairs={{0,1},{1,0},{2,3},{3,2},{4,5},{5,4},{6,7},{7,6},{8,9},{9,8},{10,11... | collective-permute-start | bytes 786440 | tf_op jit(solution)/shard_map/ppermute | solution.py:505
  27.5 4.5 %collective-permute-start.11 = (bf16[1024,128]{1,0:T(8,128)(2,1)S(1)}, bf16[1024,128]{1,0:T(8,128)(2,1)S(1)}, u32[]{:S(2)}, u32[]{:S(2)}) collective-permute-start(bf16[1024,128]{1,0:T(8,128)(2,1)S(1)} %get-tuple-element.92), channel_id=1, source_target_pairs={{0,1},{1,0},{2,3},{3,2},{4,5},{5,4},{6,7},{7,6},{8,9},{9,8},{10,11... | collective-permute-start | bytes 786440 | tf_op jit(solution)/shard_map/ppermute | solution.py:505
  30.7 24.7 %collective-permute-start.19 = (bf16[2048,128]{1,0:T(8,128)(2,1)S(1)}, bf16[2048,128]{1,0:T(8,128)(2,1)S(1)}, u32[]{:S(2)}, u32[]{:S(2)}) collective-permute-start(bf16[2048,128]{1,0:T(8,128)(2,1)S(1)} %get-tuple-element.101), channel_id=1, source_target_pairs={{8,0},{16,8},{24,16},{9,1},{17,9},{25,17},{10,2},{18,10},{26,18},{... | collective-permute-start | bytes 1572872 | tf_op jit(solution)/shard_map/ppermute | solution.py:511
  32.0 7.8 %collective-permute-start.12 = (bf16[512,128]{1,0:T(8,128)(2,1)S(1)}, bf16[512,128]{1,0:T(8,128)(2,1)S(1)}, u32[]{:S(2)}, u32[]{:S(2)}) collective-permute-start(bf16[512,128]{1,0:T(8,128)(2,1)S(1)} %get-tuple-element.96), channel_id=1, source_target_pairs={{0,2},{1,3},{2,0},{3,1},{4,6},{5,7},{6,4},{7,5},{8,10},{9,11},{10,... | collective-permute-start | bytes 393224 | tf_op jit(solution)/shard_map/ppermute | solution.py:505
  33.7 15.9 %collective-permute-start.10 = (bf16[512,256]{1,0:T(8,128)(2,1)S(1)}, bf16[512,256]{1,0:T(8,128)(2,1)S(1)}, u32[]{:S(2)}, u32[]{:S(2)}) collective-permute-start(bf16[512,256]{1,0:T(8,128)(2,1)S(1)} %get-tuple-element.89.refs_3_), channel_id=1, source_target_pairs={{0,8},{8,16},{16,24},{1,9},{9,17},{17,25},{2,10},{10,18},{18,26},{... | collective-permute-start | bytes 786440 | tf_op jit(solution)/shard_map/ppermute | solution.py:508
  38.2 9.2 %collective-permute-start.13 = (bf16[512,128]{1,0:T(8,128)(2,1)S(1)}, bf16[512,128]{1,0:T(8,128)(2,1)S(1)}, u32[]{:S(2)}, u32[]{:S(2)}) collective-permute-start(bf16[512,128]{1,0:T(8,128)(2,1)S(1)} %get-tuple-element.97), channel_id=1, source_target_pairs={{0,4},{1,5},{2,6},{3,7},{4,0},{5,1},{6,2},{7,3},{8,12},{9,13},{10,... | collective-permute-start | bytes 393224 | tf_op jit(solution)/shard_map/ppermute | solution.py:505
  39.8 7.6 %collective-permute-start.14 = (bf16[512,128]{1,0:T(8,128)(2,1)S(1)}, bf16[512,128]{1,0:T(8,128)(2,1)S(1)}, u32[]{:S(2)}, u32[]{:S(2)}) collective-permute-start(bf16[512,128]{1,0:T(8,128)(2,1)S(1)} %get-tuple-element.98), channel_id=1, source_target_pairs={{0,6},{1,7},{2,4},{3,5},{4,2},{5,3},{6,0},{7,1},{8,14},{9,15},{10,... | collective-permute-start | bytes 393224 | tf_op jit(solution)/shard_map/ppermute | solution.py:505
  50.7 1.2 %collective-permute-start.15 = (f32[16,256]{1,0:T(8,128)S(1)}, f32[16,256]{1,0:T(8,128)S(1)}, u32[]{:S(2)}, u32[]{:S(2)}) collective-permute-start(f32[16,256]{1,0:T(8,128)S(1)} %get-tuple-element.100.a_ref), channel_id=1, source_target_pairs={{0,1},{1,0},{2,3},{3,2},{4,5},{5,4},{6,7},{7,6},{8,9},{9,8},{10,11... | collective-permute-start | bytes 49160 | tf_op jit(solution)/shard_map/ppermute | solution.py:505
  51.9 4.6 %collective-permute-start.18 = (f32[16,256]{1,0:T(8,128)S(1)}, f32[16,256]{1,0:T(8,128)S(1)}, u32[]{:S(2)}, u32[]{:S(2)}) collective-permute-start(f32[16,256]{1,0:T(8,128)S(1)} %shard_map.95.refs_0_), channel_id=1, source_target_pairs={{0,6},{1,7},{2,4},{3,5},{4,2},{5,3},{6,0},{7,1},{8,14},{9,15},{10,... | collective-permute-start | bytes 49160 | tf_op jit(solution)/shard_map/ppermute | solution.py:505
  53.3 3.7 %collective-permute-start.17 = (f32[16,256]{1,0:T(8,128)S(1)}, f32[16,256]{1,0:T(8,128)S(1)}, u32[]{:S(2)}, u32[]{:S(2)}) collective-permute-start(f32[16,256]{1,0:T(8,128)S(1)} %shard_map.95.refs_0_), channel_id=1, source_target_pairs={{0,4},{1,5},{2,6},{3,7},{4,0},{5,1},{6,2},{7,3},{8,12},{9,13},{10,... | collective-permute-start | bytes 49160 | tf_op jit(solution)/shard_map/ppermute | solution.py:505
  54.9 3.7 %collective-permute-start.16 = (f32[16,256]{1,0:T(8,128)S(1)}, f32[16,256]{1,0:T(8,128)S(1)}, u32[]{:S(2)}, u32[]{:S(2)}) collective-permute-start(f32[16,256]{1,0:T(8,128)S(1)} %shard_map.95.refs_0_), channel_id=1, source_target_pairs={{0,2},{1,3},{2,0},{3,1},{4,6},{5,7},{6,4},{7,5},{8,10},{9,11},{10,... | collective-permute-start | bytes 49160 | tf_op jit(solution)/shard_map/ppermute | solution.py:505
  60.4 17.9 %collective-permute-start.20 = (bf16[2048,128]{1,0:T(8,128)(2,1)S(1)}, bf16[2048,128]{1,0:T(8,128)(2,1)S(1)}, u32[]{:S(2)}, u32[]{:S(2)}) collective-permute-start(bf16[2048,128]{1,0:T(8,128)(2,1)S(1)} %get-tuple-element.102.g_ref), channel_id=1, source_target_pairs={{8,0},{16,8},{24,16},{9,1},{17,9},{25,17},{10,2},{18,10},{26,18},{... | collective-permute-start | bytes 1572872 | tf_op jit(solution)/shard_map/ppermute | solution.py:511
  78.4 22.4 %slice-start = ((s8[8388608]{0:T(1024)(128)(4,1)}), s8[4194304]{0:T(1024)(128)(4,1)S(1)}, s32[]{:S(2)}) async-start(s8[8388608]{0:T(1024)(128)(4,1)} %bitcast), calls=%async_computation | async-start | bytes 8388608
  78.4 22.4 %slice-start.1 = ((s8[8388608]{0:T(1024)(128)(4,1)}), s8[4194304]{0:T(1024)(128)(4,1)S(1)}, s32[]{:S(2)}) async-start(s8[8388608]{0:T(1024)(128)(4,1)} %bitcast), calls=%async_computation.1 | async-start | bytes 8388608
  86.1 2.7 %collective-permute-start.21 = (bf16[1024,512]{1,0:T(8,128)(2,1)S(1)}, bf16[1024,512]{1,0:T(8,128)(2,1)S(1)}, u32[]{:S(2)}, u32[]{:S(2)}) collective-permute-start(bf16[1024,512]{1,0:T(8,128)(2,1)S(1)} %get-tuple-element.111), channel_id=1, source_target_pairs={{0,1},{1,0},{2,3},{3,2},{4,5},{5,4},{6,7},{7,6},{8,9},{9,8},{10,11... | collective-permute-start | bytes 3145736 | tf_op jit(solution)/shard_map/ppermute | solution.py:505
  86.2 14.3 %collective-permute-start.25 = (bf16[256,1024]{1,0:T(8,128)(2,1)S(1)}, bf16[256,1024]{1,0:T(8,128)(2,1)S(1)}, u32[]{:S(2)}, u32[]{:S(2)}) collective-permute-start(bf16[256,1024]{1,0:T(8,128)(2,1)S(1)} %get-tuple-element.123), channel_id=1, source_target_pairs={{0,8},{8,0},{16,24},{24,16},{1,9},{9,1},{17,25},{25,17},{2,10},{10... | collective-permute-start | bytes 1572872 | tf_op jit(solution)/shard_map/ppermute | solution.py:599
  88.9 14.8 %collective-permute-start.22 = (bf16[512,512]{1,0:T(8,128)(2,1)S(1)}, bf16[512,512]{1,0:T(8,128)(2,1)S(1)}, u32[]{:S(2)}, u32[]{:S(2)}) collective-permute-start(bf16[512,512]{1,0:T(8,128)(2,1)S(1)} %get-tuple-element.115), channel_id=1, source_target_pairs={{0,2},{1,3},{2,0},{3,1},{4,6},{5,7},{6,4},{7,5},{8,10},{9,11},{10,... | collective-permute-start | bytes 1572872 | tf_op jit(solution)/shard_map/ppermute | solution.py:505
  89.7 24.9 %collective-permute-start.23 = (bf16[512,512]{1,0:T(8,128)(2,1)S(1)}, bf16[512,512]{1,0:T(8,128)(2,1)S(1)}, u32[]{:S(2)}, u32[]{:S(2)}) collective-permute-start(bf16[512,512]{1,0:T(8,128)(2,1)S(1)} %get-tuple-element.116), channel_id=1, source_target_pairs={{0,4},{1,5},{2,6},{3,7},{4,0},{5,1},{6,2},{7,3},{8,12},{9,13},{10,... | collective-permute-start | bytes 1572872 | tf_op jit(solution)/shard_map/ppermute | solution.py:505
  90.4 26.3 %collective-permute-start.24 = (bf16[512,512]{1,0:T(8,128)(2,1)S(1)}, bf16[512,512]{1,0:T(8,128)(2,1)S(1)}, u32[]{:S(2)}, u32[]{:S(2)}) collective-permute-start(bf16[512,512]{1,0:T(8,128)(2,1)S(1)} %get-tuple-element.117), channel_id=1, source_target_pairs={{0,6},{1,7},{2,4},{3,5},{4,2},{5,3},{6,0},{7,1},{8,14},{9,15},{10,... | collective-permute-start | bytes 1572872 | tf_op jit(solution)/shard_map/ppermute | solution.py:505
  100.7 20.2 %collective-permute-start.26 = (bf16[128,1024]{1,0:T(8,128)(2,1)S(1)}, bf16[128,1024]{1,0:T(8,128)(2,1)S(1)}, u32[]{:S(2)}, u32[]{:S(2)}) collective-permute-start(bf16[128,1024]{1,0:T(8,128)(2,1)S(1)} %get-tuple-element.125), channel_id=1, source_target_pairs={{0,16},{8,24},{16,0},{24,8},{1,17},{9,25},{17,1},{25,9},{2,18},{10... | collective-permute-start | bytes 786440 | tf_op jit(solution)/shard_map/ppermute | solution.py:599
  (2 other events, 1.3 us)
where the time goes:
time: 123 us; the launch traced here: 122 us
  Pallas kernels  46.5 us (38%)
  waiting for transfers between devices  42 us (34%)
  starting transfers between devices  30.9 us (25%)
  local copies, waits for them, and re-layouts  1.33 us (1%)
    pallas_call x20, Pallas kernels, call(): pl.pallas_call(kernel, out_shape=[jax.ShapeDtypeStruct(*out) for out in o...  46.5 us
    ppermute x21, waiting for transfers between devices, swap(): return lax.ppermute(x, 'h', [(i, i ^ mask) for i in range(HEADS)])  25.6 us
    ppermute x21, starting transfers between devices, swap(): return lax.ppermute(x, 'h', [(i, i ^ mask) for i in range(HEADS)])  18.6 us
    ppermute x2, waiting for transfers between devices, between(): return lax.ppermute(x, 'g', [(i, i ^ mask) for i in range(groups)])  8.09 us
    ppermute x2, starting transfers between devices, onward(): return lax.ppermute(x, 'g', [(i, i + 1) for i in range(groups - 1)])  8.08 us
    ppermute x2, waiting for transfers between devices, backward(): return lax.ppermute(x, 'g', [(i + 1, i) for i in range(groups - 1)])  6.27 us
    ppermute x2, starting transfers between devices, backward(): return lax.ppermute(x, 'g', [(i + 1, i) for i in range(groups - 1)])  2.58 us
  transfers between devices with their start and end apart: 27, of which 15 were waited for; matrix products, arithmetic and copies ran while one was open for 0% of the time, Pallas kernels for 30%

commit v1 on v0

--- a/solution.py
+++ b/solution.py
@@ -361,10 +361,8 @@
     lax.fori_loop(0, TILES, q_tile, 0)
 
 
-def keys_kernel(
-    groups, lo_ref, at_ref, own_ref, act_ref, slope_ref, q_ref, g_ref, u_cols_ref, q_cols_ref, dq_ref, attn_ref, normed_ref, *refs
-):
-    pieces, shares, (cols_s, all_s, acc_s) = refs[:5], refs[5:-3], refs[-3:]
+def keys_kernel(lo_ref, at_ref, own_ref, act_ref, slope_ref, q_ref, g_ref, dq_ref, attn_ref, *refs):
+    pieces, (cols_ref, acc_s) = refs[:5], refs[5:]
     first = jnp.minimum(lo_ref[2 * TILES], SPAN) // CHUNK
     key = lax.broadcasted_iota(jnp.int32, (CHUNK, TILE), 0)
 
@@ -399,8 +397,12 @@
         ref[at : at + TILE, :HD] = attn_ref[rows, :]
         ref[at : at + TILE, HD : 2 * HD] = dq_ref[rows, :]
         ref[at : at + TILE, 2 * HD :] = d
-        cols_s[:, rows] = d.T
-    share = jnp.dot(cols_s[...], normed_ref[...], preferred_element_type=F32).astype(BF16)
+        cols_ref[:, rows] = d.T
+
+
+def share_kernel(groups, at_ref, u_cols_ref, q_cols_ref, cols_ref, normed_ref, *refs):
+    shares, all_s = refs[:-1], refs[-1]
+    share = jnp.dot(cols_ref[...], normed_ref[...], preferred_element_type=F32).astype(BF16)
     all_s[HD : 2 * HD, :], all_s[3 * HD :, :] = share[:HD], share[HD:]
     all_s[:HD, :] = jnp.dot(u_cols_ref[...], normed_ref[...], preferred_element_type=F32).astype(BF16)
     all_s[2 * HD : 3 * HD, :] = jnp.dot(q_cols_ref[...], normed_ref[...], preferred_element_type=F32).astype(BF16)
@@ -586,27 +588,34 @@
         [(tall_t, BF16), (tall, BF16), (wide, F32)],
         [(tall_t, BF16)],
     )
-    rows, cols = 4 * HD // groups, 4 * HD
+    rows = 4 * HD // groups
+    *pieces, cols = call(
+        keys_kernel,
+        (info[0], info[2]),
+        (dkv, act, slope, q_next, g_next, d_q, attn),
+        trade_outs(4 * HD) + [((2 * HD, SPAN), BF16)],
+        [(wide, F32)],
+    )
     outs = call(
-        functools.partial(keys_kernel, groups),
-        (info[0], info[2]),
-        (dkv, act, slope, q_next, g_next, u_cols, q_cols, d_q, attn, normed),
-        trade_outs(cols)
-        + ([((2 * rows, width), F32), ((2 * rows, width), BF16)] if groups == 4 else [((rows, width), BF16)] * groups),
-        [((2 * HD, SPAN), BF16), ((4 * HD, width), BF16), (wide, F32)],
-    )
+        functools.partial(share_kernel, groups),
+        info[2:],
+        (u_cols, q_cols, cols, normed),
+        [((2 * rows, width), F32), ((2 * rows, width), BF16)] if groups == 4 else [((rows, width), BF16)] * groups,
+        [((4 * HD, width), BF16)],
+    )
+
     def between(x, mask):
         return lax.ppermute(x, "g", [(i, i ^ mask) for i in range(groups)])
 
     if groups == 4:
-        keep, send = outs[5:]
+        keep, send = outs
         half = [((rows, width), F32), ((rows, width), BF16)]
         keep, send = call(half_kernel, (), (keep, between(send, 1)), half, limit=8)
         shares = keep, between(send, 2)
     else:
-        shares = [outs[5]] + [between(x, mask + 1) for mask, x in enumerate(outs[6:])]
-    pieces = trade(outs[:5])
-    u, slope_u = call(own_u_kernel, (), (tokens, w_in), [(own, BF16), (own, BF16)], after=(outs[0],))
+        shares = [outs[0]] + [between(x, mask + 1) for mask, x in enumerate(outs[1:])]
+    pieces = trade(pieces)
+    u, slope_u = call(own_u_kernel, (), (tokens, w_in), [(own, BF16), (own, BF16)], after=(cols,))
     d_normed = call(
         branches_kernel,
         info[2:],

time: 123 us -> 127 us (1.033); the launches traced: 122 us -> 128 us
  starting transfers between devices: 30.9 us -> 45.9 us
  waiting for transfers between devices: 42 us -> 35.9 us
  Pallas kernels: 46.5 us -> 43.8 us
    ppermute x2, starting transfers between devices: 1.6 us -> 16.6 us  [between(): return lax.ppermute(x, 'g', [(i, i ^ mask) for i in range(groups)])]
    ppermute x21, waiting for transfers between devices: 25.6 us -> 21.8 us  [swap(): return lax.ppermute(x, 'h', [(i, i ^ mask) for i in range(HEADS)])]
    ppermute x2, waiting for transfers between devices: 6.27 us -> 3.12 us  [backward(): return lax.ppermute(x, 'g', [(i + 1, i) for i in range(groups - 1)])]
    pallas_call x20 -> x21, Pallas kernels: 46.5 us -> 43.8 us  [call(): pl.pallas_call(kernel, out_shape=[jax.ShapeDtypeStruct(*out) for out in o...]
  transfers between devices with their start and end apart: 27 -> 27, of which waited for: 15 -> 13; matrix products, arithmetic and copies ran while one was open for 0% -> 0% of each run, Pallas kernels for 30% -> 31%
where the time goes in v1:
time: 127 us; the launch traced here: 128 us
  starting transfers between devices  45.9 us (36%)
  Pallas kernels  43.8 us (34%)
  waiting for transfers between devices  35.9 us (28%)
  local copies, waits for them, and re-layouts  1.34 us (1%)
    pallas_call x21, Pallas kernels, call(): pl.pallas_call(kernel, out_shape=[jax.ShapeDtypeStruct(*out) for out in o...  43.8 us
    ppermute x21, waiting for transfers between devices, swap(): return lax.ppermute(x, 'h', [(i, i ^ mask) for i in range(HEADS)])  21.8 us
    ppermute x21, starting transfers between devices, swap(): return lax.ppermute(x, 'h', [(i, i ^ mask) for i in range(HEADS)])  18.6 us
    ppermute x2, starting transfers between devices, between(): return lax.ppermute(x, 'g', [(i, i ^ mask) for i in range(groups)])  16.6 us
    ppermute x2, waiting for transfers between devices, between(): return lax.ppermute(x, 'g', [(i, i ^ mask) for i in range(groups)])  8.96 us
    ppermute x2, starting transfers between devices, onward(): return lax.ppermute(x, 'g', [(i, i + 1) for i in range(groups - 1)])  8.08 us
    ppermute x2, waiting for transfers between devices, backward(): return lax.ppermute(x, 'g', [(i + 1, i) for i in range(groups - 1)])  3.12 us
    ppermute x2, starting transfers between devices, backward(): return lax.ppermute(x, 'g', [(i + 1, i) for i in range(groups - 1)])  2.58 us
  transfers between devices with their start and end apart: 27, of which 13 were waited for; matrix products, arithmetic and copies ran while one was open for 0% of the time, Pallas kernels for 31%

profile of v1, /device:TPU:0, one launch (start us, length us, event | category | flops | bytes accessed | tf_op | source)
XLA Modules:
  0.0 127.8 jit_solution(3561608887471225352)
XLA Ops:
  1.2 2.6 %collective-permute-start.1 = (bf16[256,1024]{1,0:T(8,128)(2,1)}, bf16[256,1024]{1,0:T(8,128)(2,1)S(1)}, u32[]{:S(2)}, u32[]{:S(2)}) collective-permute-start(bf16[256,1024]{1,0:T(8,128)(2,1)} %refs_9_.1), channel_id=1, source_target_pairs={{0,4},{1,5},{2,6},{3,7},{4,0},{5,1},{6,2},{7,3},{8,12},{9,13},{10,... | collective-permute-start | bytes 1572872 | tf_op jit(solution)/shard_map/ppermute | solution.py:507
  3.8 1.5 %collective-permute-start = (bf16[256,1024]{1,0:T(8,128)(2,1)}, bf16[256,1024]{1,0:T(8,128)(2,1)S(1)}, u32[]{:S(2)}, u32[]{:S(2)}) collective-permute-start(bf16[256,1024]{1,0:T(8,128)(2,1)} %refs_9_.1), channel_id=1, source_target_pairs={{0,2},{1,3},{2,0},{3,1},{4,6},{5,7},{6,4},{7,5},{8,10},{9,11},{10,... | collective-permute-start | bytes 1572872 | tf_op jit(solution)/shard_map/ppermute | solution.py:507
  6.6 2.4 %shard_map.85 = (s32[32]{0:T(128)S(1)}, s32[32]{0:T(128)S(1)}, s32[2]{0:T(128)S(1)}, bf16[1024,512]{1,0:T(8,128)(2,1)S(1)}) custom-call(s32[16]{0:T(128)S(1)} %copy-done.3, s32[16]{0:T(128)S(1)} %copy-done.4, bf16[1024,4096]{1,0:T(8,128)(2,1)} %refs_12_.1), custom_call_target="tpu_custom_call" | custom-call | tf_op jit(solution)/shard_map/pallas_call | solution.py:489
  9.0 1.7 %shard_map.86 = (bf16[2048,1024]{1,0:T(8,128)(2,1)S(1)}, bf16[2048,512]{1,0:T(8,128)(2,1)S(1)}, bf16[2048,512]{1,0:T(8,128)(2,1)S(1)}, bf16[512,256]{1,0:T(8,128)(2,1)S(1)}) custom-call(s32[2]{0:T(128)S(1)} %get-tuple-element.66.at_ref, bf16[256,1024]{1,0:T(8,128)(2,1)S(1)} %copy-done.1, bf16[256,1024]{1,0:T(8,128)(2,1)S(1)} %collective-permute-done.2.refs_1_, ...), custom_call_target="tpu_custom_call" | custom-call | tf_op jit(solution)/shard_map/pallas_call | solution.py:489
  10.7 1.4 %shard_map.87 = (bf16[256,128]{1,0:T(8,128)(2,1)S(1)}, bf16[1024,128]{1,0:T(8,128)(2,1)S(1)}, bf16[512,128]{1,0:T(8,128)(2,1)S(1)}, bf16[512,128]{1,0:T(8,128)(2...) custom-call(s32[2]{0:T(128)S(1)} %get-tuple-element.66.at_ref, bf16[256,1024]{1,0:T(8,128)(2,1)S(1)} %copy-done.2, ...), custom_call_target="tpu_custom_call" | custom-call | tf_op jit(solution)/shard_map/pallas_call | solution.py:489
  12.1 4.4 %collective-permute-done.1.y_ref = bf16[256,1024]{1,0:T(8,128)(2,1)S(1)} collective-permute-done((bf16[256,1024]{1,0:T(8,128)(2,1)}, bf16[256,1024]{1,0:T(8,128)(2,1)S(1)}, u32[]{:S(2)}, u32[]{:S(2)}) %collective-permute-start.1) | collective-permute-done | bytes 524320 | tf_op jit(solution)/shard_map/ppermute | solution.py:507
  16.5 1.5 %collective-permute-done.x_ref = bf16[256,1024]{1,0:T(8,128)(2,1)S(1)} collective-permute-done((bf16[256,1024]{1,0:T(8,128)(2,1)}, bf16[256,1024]{1,0:T(8,128)(2,1)S(1)}, u32[]{:S(2)}, u32[]{:S(2)}) %collective-permute-start) | collective-permute-done | bytes 524320 | tf_op jit(solution)/shard_map/ppermute | solution.py:507
  18.9 1.7 %collective-permute-start.4 = (bf16[128,1024]{1,0:T(8,128)(2,1)S(1)}, bf16[128,1024]{1,0:T(8,128)(2,1)S(1)}, u32[]{:S(2)}, u32[]{:S(2)}) collective-permute-start(bf16[128,1024]{1,0:T(8,128)(2,1)S(1)} %get-tuple-element.72), channel_id=1, source_target_pairs={{0,2},{1,3},{2,0},{3,1},{4,6},{5,7},{6,4},{7,5},{8,10},{9,11},{10,... | collective-permute-start | bytes 786440 | tf_op jit(solution)/shard_map/ppermute | solution.py:507
  20.7 2.6 %shard_map.89 = (bf16[2048,1024]{1,0:T(8,128)(2,1)S(1)}, bf16[2048,512]{1,0:T(8,128)(2,1)S(1)}, bf16[2048,512]{1,0:T(8,128)(2,1)S(1)}, bf16[1536,256]{1,0:T(8,128)(2,1)S(1)}) custom-call(s32[2]{0:T(128)S(1)} %get-tuple-element.66.at_ref, bf16[256,1024]{1,0:T(8,128)(2,1)S(1)} %get-tuple-element.73.refs_0_, ...), custom_call_target="tpu_custom_call", output_to_operand_aliasing={{0}: (7, {}), {1}: (8, {}), {2}: (9, {})} | custom-call | tf_op jit(solution)/shard_map/pallas_call | solution.py:489
  23.3 3.5 %collective-permute-start.9 = (bf16[1536,256]{1,0:T(8,128)(2,1)S(1)}, bf16[1536,256]{1,0:T(8,128)(2,1)S(1)}, u32[]{:S(2)}, u32[]{:S(2)}) collective-permute-start(bf16[1536,256]{1,0:T(8,128)(2,1)S(1)} %get-tuple-element.78.refs_2_), channel_id=1, source_target_pairs={{0,8},{8,16},{16,24},{1,9},{9,17},{17,25},{2,10},{10,18},{18,26},{... | collective-permute-start | bytes 2359304 | tf_op jit(solution)/shard_map/ppermute | solution.py:510
  28.9 1.8 %shard_map.91 = (bf16[2048,1024]{1,0:T(8,128)(2,1)S(1)}, bf16[2048,512]{1,0:T(8,128)(2,1)S(1)}, bf16[2048,512]{1,0:T(8,128)(2,1)S(1)}, bf16[512,256]{1,0:T(8,128)(2,1)S(1)}, bf16[2048,128]{1,0:T(8,128)(2,1)S(1)}) custom-call(s32[2]{0:T(128)S(1)} %get-tuple-element.66.at_ref, ...), custom_call_target="tpu_custom_call", output_to_operand_aliasing={{0}: (6, {}), {1}: (7, {}), {2}: (8, {})} | custom-call | tf_op jit(solution)/shard_map/pallas_call | solution.py:489
  32.0 1.7 %collective-permute-start.12 = (bf16[512,128]{1,0:T(8,128)(2,1)S(1)}, bf16[512,128]{1,0:T(8,128)(2,1)S(1)}, u32[]{:S(2)}, u32[]{:S(2)}) collective-permute-start(bf16[512,128]{1,0:T(8,128)(2,1)S(1)} %get-tuple-element.97), channel_id=1, source_target_pairs={{0,2},{1,3},{2,0},{3,1},{4,6},{5,7},{6,4},{7,5},{8,10},{9,11},{10,... | collective-permute-start | bytes 393224 | tf_op jit(solution)/shard_map/ppermute | solution.py:507
  33.7 4.5 %collective-permute-start.10 = (bf16[512,256]{1,0:T(8,128)(2,1)S(1)}, bf16[512,256]{1,0:T(8,128)(2,1)S(1)}, u32[]{:S(2)}, u32[]{:S(2)}) collective-permute-start(bf16[512,256]{1,0:T(8,128)(2,1)S(1)} %get-tuple-element.90.refs_3_), channel_id=1, source_target_pairs={{0,8},{8,16},{16,24},{1,9},{9,17},{17,25},{2,10},{10,18},{18,26},{... | collective-permute-start | bytes 786440 | tf_op jit(solution)/shard_map/ppermute | solution.py:510
  38.2 1.6 %collective-permute-start.13 = (bf16[512,128]{1,0:T(8,128)(2,1)S(1)}, bf16[512,128]{1,0:T(8,128)(2,1)S(1)}, u32[]{:S(2)}, u32[]{:S(2)}) collective-permute-start(bf16[512,128]{1,0:T(8,128)(2,1)S(1)} %get-tuple-element.98), channel_id=1, source_target_pairs={{0,4},{1,5},{2,6},{3,7},{4,0},{5,1},{6,2},{7,3},{8,12},{9,13},{10,... | collective-permute-start | bytes 393224 | tf_op jit(solution)/shard_map/ppermute | solution.py:507
  40.2 7.3 %shard_map.92 = (f32[2048,128]{1,0:T(8,128)S(1)}, bf16[128,2048]{1,0:T(8,128)(2,1)S(1)}, bf16[128,2048]{1,0:T(8,128)(2,1)S(1)}, bf16[128,2048]{1,0:T(8,128)(2,1)S(1)}) custom-call(s32[32]{0:T(128)S(1)} %get-tuple-element.67.lo_ref, s32[32]{0:T(128)S(1)} %get-tuple-element.85.nv_ref, bf16[2048,512]{1,0:T(8,128)(2,1)S(1)} %get-tuple-element.84.act_ref, ...), custom_call_target="tpu_custom_call" | custom-call | tf_op jit(solution)/shard_map/pallas_call | solution.py:489
  47.5 2.0 %collective-permute-done.10.kvb_ref = bf16[512,256]{1,0:T(8,128)(2,1)S(1)} collective-permute-done((bf16[512,256]{1,0:T(8,128)(2,1)S(1)}, bf16[512,256]{1,0:T(8,128)(2,1)S(1)}, u32[]{:S(2)}, u32[]{:S(2)}) %collective-permute-start.10) | collective-permute-done | bytes 262176 | tf_op jit(solution)/shard_map/ppermute | solution.py:510
  51.9 1.4 %collective-permute-start.18 = (f32[16,256]{1,0:T(8,128)S(1)}, f32[16,256]{1,0:T(8,128)S(1)}, u32[]{:S(2)}, u32[]{:S(2)}) collective-permute-start(f32[16,256]{1,0:T(8,128)S(1)} %shard_map.95.refs_0_), channel_id=1, source_target_pairs={{0,6},{1,7},{2,4},{3,5},{4,2},{5,3},{6,0},{7,1},{8,14},{9,15},{10,... | collective-permute-start | bytes 49160 | tf_op jit(solution)/shard_map/ppermute | solution.py:507
  53.4 1.5 %collective-permute-start.17 = (f32[16,256]{1,0:T(8,128)S(1)}, f32[16,256]{1,0:T(8,128)S(1)}, u32[]{:S(2)}, u32[]{:S(2)}) collective-permute-start(f32[16,256]{1,0:T(8,128)S(1)} %shard_map.95.refs_0_), channel_id=1, source_target_pairs={{0,4},{1,5},{2,6},{3,7},{4,0},{5,1},{6,2},{7,3},{8,12},{9,13},{10,... | collective-permute-start | bytes 49160 | tf_op jit(solution)/shard_map/ppermute | solution.py:507
  57.1 1.5 %collective-permute-done.16.refs_1_ = f32[16,256]{1,0:T(8,128)S(1)} collective-permute-done((f32[16,256]{1,0:T(8,128)S(1)}, f32[16,256]{1,0:T(8,128)S(1)}, u32[]{:S(2)}, u32[]{:S(2)}) %collective-permute-start.16) | collective-permute-done | bytes 16416 | tf_op jit(solution)/shard_map/ppermute | solution.py:507
  58.6 1.9 %shard_map.96 = (bf16[2048,128]{1,0:T(8,128)(2,1)S(1)}, bf16[128,2048]{1,0:T(8,128)(2,1)S(1)}) custom-call(s32[32]{0:T(128)S(1)} %get-tuple-element.85.nv_ref, s32[2]{0:T(128)S(1)} %get-tuple-element.66.at_ref, bf16[2048,512]{1,0:T(8,128)(2,1)S(1)} %get-tuple-element.84.act_ref, bf16[2048,512]{1,0:T(8,128)(2,1)S(1)} %get-tuple-element.86.slope_ref, ...), custom_call_target="tpu_custom_call" | custom-call | tf_op jit(solution)/shard_map/pallas_call | solution.py:489
  60.5 1.3 %collective-permute-start.20 = (bf16[2048,128]{1,0:T(8,128)(2,1)S(1)}, bf16[2048,128]{1,0:T(8,128)(2,1)S(1)}, u32[]{:S(2)}, u32[]{:S(2)}) collective-permute-start(bf16[2048,128]{1,0:T(8,128)(2,1)S(1)} %get-tuple-element.103.g_ref), channel_id=1, source_target_pairs={{8,0},{16,8},{24,16},{9,1},{17,9},{25,17},{10,2},{18,10},{26,18},{... | collective-permute-start | bytes 1572872 | tf_op jit(solution)/shard_map/ppermute | solution.py:513
  61.8 10.6 %shard_map.97 = (bf16[128,2048]{1,0:T(8,128)(2,1)S(1)}, bf16[2048,128]{1,0:T(8,128)(2,1)S(1)}, f32[2048,256]{1,0:T(8,128)S(1)}) custom-call(s32[32]{0:T(128)S(1)} %get-tuple-element.67.lo_ref, bf16[2048,512]{1,0:T(8,128)(2,1)S(1)} %get-tuple-element.84.act_ref, bf16[128,2048]{1,0:T(8,128)(2,1)S(1)} %get-tuple-element.87.slope_qt_ref, ...), custom_call_target="tpu_custom_call" | custom-call | tf_op jit(solution)/shard_map/pallas_call | solution.py:489
  72.4 3.1 %collective-permute-done.20.g_ref = bf16[2048,128]{1,0:T(8,128)(2,1)S(1)} collective-permute-done((bf16[2048,128]{1,0:T(8,128)(2,1)S(1)}, bf16[2048,128]{1,0:T(8,128)(2,1)S(1)}, u32[]{:S(2)}, u32[]{:S(2)}) %collective-permute-start.20) | collective-permute-done | bytes 524320 | tf_op jit(solution)/shard_map/ppermute | solution.py:513
  75.6 1.5 %shard_map.98 = (bf16[256,512]{1,0:T(8,128)(2,1)S(1)}, bf16[1024,512]{1,0:T(8,128)(2,1)S(1)}, bf16[512,512]{1,0:T(8,128)(2,1)S(1)}, bf16[512,512]{1,0:T(8,128)(2...) custom-call(s32[32]{0:T(128)S(1)} %get-tuple-element.67.lo_ref, s32[2]{0:T(128)S(1)} %get-tuple-element.66.at_ref, ...), custom_call_target="tpu_custom_call" | custom-call | tf_op jit(solution)/shard_map/pallas_call | solution.py:489
  77.2 3.1 %shard_map.103 = (f32[256,1024]{1,0:T(8,128)S(1)}, bf16[256,1024]{1,0:T(8,128)(2,1)S(1)}) custom-call(s32[2]{0:T(128)S(1)} %get-tuple-element.66.at_ref, bf16[128,2048]{1,0:T(8,128)(2,1)S(1)} %get-tuple-element.121.u_cols_ref, bf16[128,2048]{1,0:T(8,128)(2,1)S(1)} %get-tuple-element.122.q_cols_ref, ...), custom_call_target="tpu_custom_call" | custom-call | tf_op jit(solution)/shard_map/pallas_call | solution.py:489
  80.2 14.7 %collective-permute-start.25 = (bf16[256,1024]{1,0:T(8,128)(2,1)S(1)}, bf16[256,1024]{1,0:T(8,128)(2,1)S(1)}, u32[]{:S(2)}, u32[]{:S(2)}) collective-permute-start(bf16[256,1024]{1,0:T(8,128)(2,1)S(1)} %get-tuple-element.125), channel_id=1, source_target_pairs={{0,8},{8,0},{16,24},{24,16},{1,9},{9,1},{17,25},{25,17},{2,10},{10... | collective-permute-start | bytes 1572872 | tf_op jit(solution)/shard_map/ppermute | solution.py:608
  96.5 2.0 %collective-permute-start.24 = (bf16[512,512]{1,0:T(8,128)(2,1)S(1)}, bf16[512,512]{1,0:T(8,128)(2,1)S(1)}, u32[]{:S(2)}, u32[]{:S(2)}) collective-permute-start(bf16[512,512]{1,0:T(8,128)(2,1)S(1)} %get-tuple-element.115), channel_id=1, source_target_pairs={{0,6},{1,7},{2,4},{3,5},{4,2},{5,3},{6,0},{7,1},{8,14},{9,15},{10,... | collective-permute-start | bytes 1572872 | tf_op jit(solution)/shard_map/ppermute | solution.py:507
  98.5 9.0 %collective-permute-done.25.got_ref = bf16[256,1024]{1,0:T(8,128)(2,1)S(1)} collective-permute-done((bf16[256,1024]{1,0:T(8,128)(2,1)S(1)}, bf16[256,1024]{1,0:T(8,128)(2,1)S(1)}, u32[]{:S(2)}, u32[]{:S(2)}) %collective-permute-start.25) | collective-permute-done | bytes 524320 | tf_op jit(solution)/shard_map/ppermute | solution.py:608
  107.6 2.0 %collective-permute-start.26 = (bf16[128,1024]{1,0:T(8,128)(2,1)S(1)}, bf16[128,1024]{1,0:T(8,128)(2,1)S(1)}, u32[]{:S(2)}, u32[]{:S(2)}) collective-permute-start(bf16[128,1024]{1,0:T(8,128)(2,1)S(1)} %get-tuple-element.127), channel_id=1, source_target_pairs={{0,16},{8,24},{16,0},{24,8},{1,17},{9,25},{17,1},{25,9},{2,18},{10... | collective-permute-start | bytes 786440 | tf_op jit(solution)/shard_map/ppermute | solution.py:608
  110.6 10.1 %collective-permute-done.23.refs_3_ = bf16[512,512]{1,0:T(8,128)(2,1)S(1)} collective-permute-done((bf16[512,512]{1,0:T(8,128)(2,1)S(1)}, bf16[512,512]{1,0:T(8,128)(2,1)S(1)}, u32[]{:S(2)}, u32[]{:S(2)}) %collective-permute-start.23) | collective-permute-done | bytes 524320 | tf_op jit(solution)/shard_map/ppermute | solution.py:507
  120.7 2.2 %shard_map.100.refs_5_ = f32[256,1024]{1,0:T(8,128)S(1)} custom-call(s32[2]{0:T(128)S(1)} %get-tuple-element.66.at_ref, bf16[256,512]{1,0:T(8,128)(2,1)S(1)} %get-tuple-element.108.refs_0_, bf16[1024,512]{1,0:T(8,128)(2,1)S(1)} %collective-permute-done.21.other_ref.refs_1_, bf16[512,512]{1,0:T(8,128)(2,1)S(1)} %collective-permute-done.22.refs_2_, ...), custom_call_target="tpu_custom_call" | custom-call | tf_op jit(solution)/shard_map/pallas_call | solution.py:489
  122.9 4.1 %shard_map.102 = (bf16[256,1024]{1,0:T(8,128)(2,1)}, bf16[256,1024]{1,0:T(8,128)(2,1)}, f32[8,128]{1,0:T(8,128)S(1)}) custom-call(s32[2]{0:T(128)S(1)} %get-tuple-element.66.at_ref, bf16[256,512]{1,0:T(8,128)(2,1)S(1)} %get-tuple-element.108.refs_0_, bf16[1024,512]{1,0:T(8,128)(2,1)S(1)} %collective-permute-done.21.other_ref.refs_1_, ...), custom_call_target="tpu_custom_call" | custom-call | tf_op jit(solution)/shard_map/pallas_call | solution.py:489
  (58 shorter events, 14.8 us)
Async XLA Ops:
  0.6 8.4 %copy-start.1 = (bf16[256,1024]{1,0:T(8,128)(2,1)S(1)}, bf16[256,1024]{1,0:T(8,128)(2,1)}, u32[]{:S(2)}) copy-start(bf16[256,1024]{1,0:T(8,128)(2,1)} %refs_9_.1) | copy-start | bytes 1572868
  0.6 8.3 %collective-permute-start.2 = (bf16[256,1024]{1,0:T(8,128)(2,1)}, bf16[256,1024]{1,0:T(8,128)(2,1)S(1)}, u32[]{:S(2)}, u32[]{:S(2)}) collective-permute-start(bf16[256,1024]{1,0:T(8,128)(2,1)} %refs_9_.1), channel_id=1, source_target_pairs={{0,1},{1,0},{2,3},{3,2},{4,5},{5,4},{6,7},{7,6},{8,9},{9,8},{10,11... | collective-permute-start | bytes 1572872 | tf_op jit(solution)/shard_map/ppermute | solution.py:507
  1.2 15.3 %collective-permute-start.1 = (bf16[256,1024]{1,0:T(8,128)(2,1)}, bf16[256,1024]{1,0:T(8,128)(2,1)S(1)}, u32[]{:S(2)}, u32[]{:S(2)}) collective-permute-start(bf16[256,1024]{1,0:T(8,128)(2,1)} %refs_9_.1), channel_id=1, source_target_pairs={{0,4},{1,5},{2,6},{3,7},{4,0},{5,1},{6,2},{7,3},{8,12},{9,13},{10,... | collective-permute-start | bytes 1572872 | tf_op jit(solution)/shard_map/ppermute | solution.py:507
  3.8 14.2 %collective-permute-start = (bf16[256,1024]{1,0:T(8,128)(2,1)}, bf16[256,1024]{1,0:T(8,128)(2,1)S(1)}, u32[]{:S(2)}, u32[]{:S(2)}) collective-permute-start(bf16[256,1024]{1,0:T(8,128)(2,1)} %refs_9_.1), channel_id=1, source_target_pairs={{0,2},{1,3},{2,0},{3,1},{4,6},{5,7},{6,4},{7,5},{8,10},{9,11},{10,... | collective-permute-start | bytes 1572872 | tf_op jit(solution)/shard_map/ppermute | solution.py:507
  6.6 4.1 %copy-start.2 = (bf16[256,1024]{1,0:T(8,128)(2,1)S(1)}, bf16[256,1024]{1,0:T(8,128)(2,1)}, u32[]{:S(2)}) copy-start(bf16[256,1024]{1,0:T(8,128)(2,1)} %refs_10_.1) | copy-start | bytes 1572868
  9.0 1.7 %copy-start = (bf16[1024,1024]{1,0:T(8,128)(2,1)S(1)}, bf16[1024,1024]{1,0:T(8,128)(2,1)}, u32[]{:S(2)}) copy-start(bf16[1024,1024]{1,0:T(8,128)(2,1)} %refs_11_.1) | copy-start | bytes 6291460
  18.0 2.6 %collective-permute-start.5 = (bf16[256,1024]{1,0:T(8,128)(2,1)S(1)}, bf16[256,1024]{1,0:T(8,128)(2,1)S(1)}, u32[]{:S(2)}, u32[]{:S(2)}) collective-permute-start(bf16[256,1024]{1,0:T(8,128)(2,1)S(1)} %get-tuple-element.73.refs_0_), channel_id=1, source_target_pairs={{0,1},{1,0},{2,3},{3,2},{4,5},{5,4},{6,7},{7,6},{8,9},{9,8},{10,11... | collective-permute-start | bytes 1572872 | tf_op jit(solution)/shard_map/ppermute | solution.py:507
  18.1 2.6 %collective-permute-start.6 = (bf16[256,1024]{1,0:T(8,128)(2,1)S(1)}, bf16[256,1024]{1,0:T(8,128)(2,1)S(1)}, u32[]{:S(2)}, u32[]{:S(2)}) collective-permute-start(bf16[256,1024]{1,0:T(8,128)(2,1)S(1)} %get-tuple-element.74.refs_2_), channel_id=1, source_target_pairs={{0,1},{1,0},{2,3},{3,2},{4,5},{5,4},{6,7},{7,6},{8,9},{9,8},{10,11... | collective-permute-start | bytes 1572872 | tf_op jit(solution)/shard_map/ppermute | solution.py:507
  18.6 8.3 %collective-permute-start.3 = (bf16[128,1024]{1,0:T(8,128)(2,1)S(1)}, bf16[128,1024]{1,0:T(8,128)(2,1)S(1)}, u32[]{:S(2)}, u32[]{:S(2)}) collective-permute-start(bf16[128,1024]{1,0:T(8,128)(2,1)S(1)} %get-tuple-element.71), channel_id=1, source_target_pairs={{0,4},{1,5},{2,6},{3,7},{4,0},{5,1},{6,2},{7,3},{8,12},{9,13},{10,... | collective-permute-start | bytes 786440 | tf_op jit(solution)/shard_map/ppermute | solution.py:507
  18.9 8.0 %collective-permute-start.4 = (bf16[128,1024]{1,0:T(8,128)(2,1)S(1)}, bf16[128,1024]{1,0:T(8,128)(2,1)S(1)}, u32[]{:S(2)}, u32[]{:S(2)}) collective-permute-start(bf16[128,1024]{1,0:T(8,128)(2,1)S(1)} %get-tuple-element.72), channel_id=1, source_target_pairs={{0,2},{1,3},{2,0},{3,1},{4,6},{5,7},{6,4},{7,5},{8,10},{9,11},{10,... | collective-permute-start | bytes 786440 | tf_op jit(solution)/shard_map/ppermute | solution.py:507
  23.3 26.2 %collective-permute-start.9 = (bf16[1536,256]{1,0:T(8,128)(2,1)S(1)}, bf16[1536,256]{1,0:T(8,128)(2,1)S(1)}, u32[]{:S(2)}, u32[]{:S(2)}) collective-permute-start(bf16[1536,256]{1,0:T(8,128)(2,1)S(1)} %get-tuple-element.78.refs_2_), channel_id=1, source_target_pairs={{0,8},{8,16},{16,24},{1,9},{9,17},{17,25},{2,10},{10,18},{18,26},{... | collective-permute-start | bytes 2359304 | tf_op jit(solution)/shard_map/ppermute | solution.py:510
  26.9 1.6 %collective-permute-start.7 = (bf16[128,1024]{1,0:T(8,128)(2,1)S(1)}, bf16[128,1024]{1,0:T(8,128)(2,1)S(1)}, u32[]{:S(2)}, u32[]{:S(2)}) collective-permute-start(bf16[128,1024]{1,0:T(8,128)(2,1)S(1)} %get-tuple-element.79.refs_0_), channel_id=1, source_target_pairs={{0,1},{1,0},{2,3},{3,2},{4,5},{5,4},{6,7},{7,6},{8,9},{9,8},{10,11... | collective-permute-start | bytes 786440 | tf_op jit(solution)/shard_map/ppermute | solution.py:507
  27.0 1.9 %collective-permute-start.8 = (bf16[128,1024]{1,0:T(8,128)(2,1)S(1)}, bf16[128,1024]{1,0:T(8,128)(2,1)S(1)}, u32[]{:S(2)}, u32[]{:S(2)}) collective-permute-start(bf16[128,1024]{1,0:T(8,128)(2,1)S(1)} %get-tuple-element.80.refs_1_), channel_id=1, source_target_pairs={{0,1},{1,0},{2,3},{3,2},{4,5},{5,4},{6,7},{7,6},{8,9},{9,8},{10,11... | collective-permute-start | bytes 786440 | tf_op jit(solution)/shard_map/ppermute | solution.py:507
  27.5 4.5 %collective-permute-start.11 = (bf16[1024,128]{1,0:T(8,128)(2,1)S(1)}, bf16[1024,128]{1,0:T(8,128)(2,1)S(1)}, u32[]{:S(2)}, u32[]{:S(2)}) collective-permute-start(bf16[1024,128]{1,0:T(8,128)(2,1)S(1)} %get-tuple-element.93), channel_id=1, source_target_pairs={{0,1},{1,0},{2,3},{3,2},{4,5},{5,4},{6,7},{7,6},{8,9},{9,8},{10,11... | collective-permute-start | bytes 786440 | tf_op jit(solution)/shard_map/ppermute | solution.py:507
  30.7 24.8 %collective-permute-start.19 = (bf16[2048,128]{1,0:T(8,128)(2,1)S(1)}, bf16[2048,128]{1,0:T(8,128)(2,1)S(1)}, u32[]{:S(2)}, u32[]{:S(2)}) collective-permute-start(bf16[2048,128]{1,0:T(8,128)(2,1)S(1)} %get-tuple-element.102), channel_id=1, source_target_pairs={{8,0},{16,8},{24,16},{9,1},{17,9},{25,17},{10,2},{18,10},{26,18},{... | collective-permute-start | bytes 1572872 | tf_op jit(solution)/shard_map/ppermute | solution.py:513
  32.0 7.8 %collective-permute-start.12 = (bf16[512,128]{1,0:T(8,128)(2,1)S(1)}, bf16[512,128]{1,0:T(8,128)(2,1)S(1)}, u32[]{:S(2)}, u32[]{:S(2)}) collective-permute-start(bf16[512,128]{1,0:T(8,128)(2,1)S(1)} %get-tuple-element.97), channel_id=1, source_target_pairs={{0,2},{1,3},{2,0},{3,1},{4,6},{5,7},{6,4},{7,5},{8,10},{9,11},{10,... | collective-permute-start | bytes 393224 | tf_op jit(solution)/shard_map/ppermute | solution.py:507
  33.7 15.9 %collective-permute-start.10 = (bf16[512,256]{1,0:T(8,128)(2,1)S(1)}, bf16[512,256]{1,0:T(8,128)(2,1)S(1)}, u32[]{:S(2)}, u32[]{:S(2)}) collective-permute-start(bf16[512,256]{1,0:T(8,128)(2,1)S(1)} %get-tuple-element.90.refs_3_), channel_id=1, source_target_pairs={{0,8},{8,16},{16,24},{1,9},{9,17},{17,25},{2,10},{10,18},{18,26},{... | collective-permute-start | bytes 786440 | tf_op jit(solution)/shard_map/ppermute | solution.py:510
  38.2 9.3 %collective-permute-start.13 = (bf16[512,128]{1,0:T(8,128)(2,1)S(1)}, bf16[512,128]{1,0:T(8,128)(2,1)S(1)}, u32[]{:S(2)}, u32[]{:S(2)}) collective-permute-start(bf16[512,128]{1,0:T(8,128)(2,1)S(1)} %get-tuple-element.98), channel_id=1, source_target_pairs={{0,4},{1,5},{2,6},{3,7},{4,0},{5,1},{6,2},{7,3},{8,12},{9,13},{10,... | collective-permute-start | bytes 393224 | tf_op jit(solution)/shard_map/ppermute | solution.py:507
  39.8 7.7 %collective-permute-start.14 = (bf16[512,128]{1,0:T(8,128)(2,1)S(1)}, bf16[512,128]{1,0:T(8,128)(2,1)S(1)}, u32[]{:S(2)}, u32[]{:S(2)}) collective-permute-start(bf16[512,128]{1,0:T(8,128)(2,1)S(1)} %get-tuple-element.99), channel_id=1, source_target_pairs={{0,6},{1,7},{2,4},{3,5},{4,2},{5,3},{6,0},{7,1},{8,14},{9,15},{10,... | collective-permute-start | bytes 393224 | tf_op jit(solution)/shard_map/ppermute | solution.py:507
  50.7 1.2 collective-permute-start.15
  51.9 4.6 %collective-permute-start.18 = (f32[16,256]{1,0:T(8,128)S(1)}, f32[16,256]{1,0:T(8,128)S(1)}, u32[]{:S(2)}, u32[]{:S(2)}) collective-permute-start(f32[16,256]{1,0:T(8,128)S(1)} %shard_map.95.refs_0_), channel_id=1, source_target_pairs={{0,6},{1,7},{2,4},{3,5},{4,2},{5,3},{6,0},{7,1},{8,14},{9,15},{10,... | collective-permute-start | bytes 49160 | tf_op jit(solution)/shard_map/ppermute | solution.py:507
  53.4 3.7 %collective-permute-start.17 = (f32[16,256]{1,0:T(8,128)S(1)}, f32[16,256]{1,0:T(8,128)S(1)}, u32[]{:S(2)}, u32[]{:S(2)}) collective-permute-start(f32[16,256]{1,0:T(8,128)S(1)} %shard_map.95.refs_0_), channel_id=1, source_target_pairs={{0,4},{1,5},{2,6},{3,7},{4,0},{5,1},{6,2},{7,3},{8,12},{9,13},{10,... | collective-permute-start | bytes 49160 | tf_op jit(solution)/shard_map/ppermute | solution.py:507
  54.9 3.7 %collective-permute-start.16 = (f32[16,256]{1,0:T(8,128)S(1)}, f32[16,256]{1,0:T(8,128)S(1)}, u32[]{:S(2)}, u32[]{:S(2)}) collective-permute-start(f32[16,256]{1,0:T(8,128)S(1)} %shard_map.95.refs_0_), channel_id=1, source_target_pairs={{0,2},{1,3},{2,0},{3,1},{4,6},{5,7},{6,4},{7,5},{8,10},{9,11},{10,... | collective-permute-start | bytes 49160 | tf_op jit(solution)/shard_map/ppermute | solution.py:507
  60.5 15.1 %collective-permute-start.20 = (bf16[2048,128]{1,0:T(8,128)(2,1)S(1)}, bf16[2048,128]{1,0:T(8,128)(2,1)S(1)}, u32[]{:S(2)}, u32[]{:S(2)}) collective-permute-start(bf16[2048,128]{1,0:T(8,128)(2,1)S(1)} %get-tuple-element.103.g_ref), channel_id=1, source_target_pairs={{8,0},{16,8},{24,16},{9,1},{17,9},{25,17},{10,2},{18,10},{26,18},{... | collective-permute-start | bytes 1572872 | tf_op jit(solution)/shard_map/ppermute | solution.py:513
  75.6 34.0 %slice-start = ((s8[8388608]{0:T(1024)(128)(4,1)}), s8[4194304]{0:T(1024)(128)(4,1)S(1)}, s32[]{:S(2)}) async-start(s8[8388608]{0:T(1024)(128)(4,1)} %bitcast), calls=%async_computation | async-start | bytes 8388608
  77.1 17.8 %collective-permute-start.21 = (bf16[1024,512]{1,0:T(8,128)(2,1)S(1)}, bf16[1024,512]{1,0:T(8,128)(2,1)S(1)}, u32[]{:S(2)}, u32[]{:S(2)}) collective-permute-start(bf16[1024,512]{1,0:T(8,128)(2,1)S(1)} %get-tuple-element.109), channel_id=1, source_target_pairs={{0,1},{1,0},{2,3},{3,2},{4,5},{5,4},{6,7},{7,6},{8,9},{9,8},{10,11... | collective-permute-start | bytes 3145736 | tf_op jit(solution)/shard_map/ppermute | solution.py:507
  77.2 32.4 %slice-start.1 = ((s8[8388608]{0:T(1024)(128)(4,1)}), s8[4194304]{0:T(1024)(128)(4,1)S(1)}, s32[]{:S(2)}) async-start(s8[8388608]{0:T(1024)(128)(4,1)} %bitcast), calls=%async_computation.1 | async-start | bytes 8388608
  80.2 27.3 %collective-permute-start.25 = (bf16[256,1024]{1,0:T(8,128)(2,1)S(1)}, bf16[256,1024]{1,0:T(8,128)(2,1)S(1)}, u32[]{:S(2)}, u32[]{:S(2)}) collective-permute-start(bf16[256,1024]{1,0:T(8,128)(2,1)S(1)} %get-tuple-element.125), channel_id=1, source_target_pairs={{0,8},{8,0},{16,24},{24,16},{1,9},{9,1},{17,25},{25,17},{2,10},{10... | collective-permute-start | bytes 1572872 | tf_op jit(solution)/shard_map/ppermute | solution.py:608
  95.0 15.7 %collective-permute-start.22 = (bf16[512,512]{1,0:T(8,128)(2,1)S(1)}, bf16[512,512]{1,0:T(8,128)(2,1)S(1)}, u32[]{:S(2)}, u32[]{:S(2)}) collective-permute-start(bf16[512,512]{1,0:T(8,128)(2,1)S(1)} %get-tuple-element.113), channel_id=1, source_target_pairs={{0,2},{1,3},{2,0},{3,1},{4,6},{5,7},{6,4},{7,5},{8,10},{9,11},{10,... | collective-permute-start | bytes 1572872 | tf_op jit(solution)/shard_map/ppermute | solution.py:507
  95.7 25.0 %collective-permute-start.23 = (bf16[512,512]{1,0:T(8,128)(2,1)S(1)}, bf16[512,512]{1,0:T(8,128)(2,1)S(1)}, u32[]{:S(2)}, u32[]{:S(2)}) collective-permute-start(bf16[512,512]{1,0:T(8,128)(2,1)S(1)} %get-tuple-element.114), channel_id=1, source_target_pairs={{0,4},{1,5},{2,6},{3,7},{4,0},{5,1},{6,2},{7,3},{8,12},{9,13},{10,... | collective-permute-start | bytes 1572872 | tf_op jit(solution)/shard_map/ppermute | solution.py:507
  96.5 26.4 %collective-permute-start.24 = (bf16[512,512]{1,0:T(8,128)(2,1)S(1)}, bf16[512,512]{1,0:T(8,128)(2,1)S(1)}, u32[]{:S(2)}, u32[]{:S(2)}) collective-permute-start(bf16[512,512]{1,0:T(8,128)(2,1)S(1)} %get-tuple-element.115), channel_id=1, source_target_pairs={{0,6},{1,7},{2,4},{3,5},{4,2},{5,3},{6,0},{7,1},{8,14},{9,15},{10,... | collective-permute-start | bytes 1572872 | tf_op jit(solution)/shard_map/ppermute | solution.py:507
  107.6 19.4 %collective-permute-start.26 = (bf16[128,1024]{1,0:T(8,128)(2,1)S(1)}, bf16[128,1024]{1,0:T(8,128)(2,1)S(1)}, u32[]{:S(2)}, u32[]{:S(2)}) collective-permute-start(bf16[128,1024]{1,0:T(8,128)(2,1)S(1)} %get-tuple-element.127), channel_id=1, source_target_pairs={{0,16},{8,24},{16,0},{24,8},{1,17},{9,25},{17,1},{25,9},{2,18},{10... | collective-permute-start | bytes 786440 | tf_op jit(solution)/shard_map/ppermute | solution.py:608
  (2 other events, 1.3 us)

commit v2 on v1

--- a/solution.py
+++ b/solution.py
@@ -70,6 +70,14 @@
     return jnp.concatenate(parts, axis=1 - dim)
 
 
+def with_mask(visible, mask, body, carry):
+    return lax.cond(visible, lambda c: body(None, c), lambda c: body(mask(), c), carry)
+
+
+def latest_start(t, lo_ref):
+    return jnp.maximum(lo_ref[2 * t], lo_ref[2 * t + 1])
+
+
 def valid_rows(t, nv_ref):
     row = lax.broadcasted_iota(jnp.int32, (TILE, 1), 0)
     return (row & (BLK - 1)) < by_half(t, nv_ref, (TILE, 1), 0)
@@ -196,7 +204,8 @@
 
 def weigh(q, kt, v, mask):
     s = jnp.dot(q, kt, preferred_element_type=F32)
-    w = jnp.where(mask, s * sigmoid(s), 0.0).astype(BF16)
+    w = s * sigmoid(s)
+    w = (w if mask is None else jnp.where(mask, w, 0.0)).astype(BF16)
     return jnp.dot(w, v, preferred_element_type=F32)
 
 
@@ -211,8 +220,14 @@
         q = act_ref[rows_at(t), Q]
 
         def keys(at, size, acc):
-            mask = from_start(t, lo_ref, at, col[:, :size], 1) & ((col - row)[:, :size] <= t * TILE - at)
-            return acc + weigh(q, kt_ref[:, pl.ds(at, size)], act_ref[pl.ds(at, size), V], mask)
+            def mask():
+                return from_start(t, lo_ref, at, col[:, :size], 1) & ((col - row)[:, :size] <= t * TILE - at)
+
+            def body(mask, acc):
+                return acc + weigh(q, kt_ref[:, pl.ds(at, size)], act_ref[pl.ds(at, size), V], mask)
+
+            visible = (at >= latest_start(t, lo_ref)) & (at + size <= t * TILE)
+            return with_mask(visible, mask, body, acc)
 
         first = jnp.maximum(lo_ref[2 * t], 0) // TILE
         acc = tiles_back(t, first, keys, jnp.zeros((TILE, HD), F32))
@@ -253,8 +268,13 @@
         q = act_ref[rows_at(t), Q]
 
         def k_chunk(c, acc):
-            mask = from_start(t, lo_ref, c * CHUNK - SPAN, col, 1)
-            return acc + weigh(q, kt_ref[:, chunk_at(c)], kv_ref[chunk_at(c), :HD], mask)
+            def mask():
+                return from_start(t, lo_ref, c * CHUNK - SPAN, col, 1)
+
+            def body(mask, acc):
+                return acc + weigh(q, kt_ref[:, chunk_at(c)], kv_ref[chunk_at(c), :HD], mask)
+
+            return with_mask(c * CHUNK - SPAN >= latest_start(t, lo_ref), mask, body, acc)
 
         start = (lo_ref[2 * t] + SPAN) // CHUNK
         acc = lax.fori_loop(start, CHUNKS, k_chunk, jnp.zeros((TILE, HD), F32))
@@ -301,10 +321,13 @@
 
 def back_scores(qt, k, v, gt, mask):
     s = jnp.dot(k, qt, preferred_element_type=F32)
-    sig = jnp.where(mask, sigmoid(s), 0.0)
+    sig = sigmoid(s)
+    if mask is not None:
+        sig = jnp.where(mask, sig, 0.0)
+    w = s * sig
     dw = jnp.dot(v, gt, preferred_element_type=F32)
-    ds = dw * sig * (1.0 + (s * SCALE) * (1.0 - sig))
-    return (s * sig).astype(BF16), ds.astype(BF16)
+    ds = dw * (sig + SCALE * (w - w * sig))
+    return w.astype(BF16), ds.astype(BF16)
 
 
 def cotangent_kernel(nv_ref, at_ref, act_ref, slope_ref, attn_ref, *refs):
@@ -336,17 +359,30 @@
 
         def far_chunk(c, dqt):
             at = chunk_at(c)
-            mask = from_start(t, lo_ref, c * CHUNK - SPAN, key, 0)
-            ds = back_scores(qt, kv_ref[at, HD:], kv_ref[at, :HD], gt, mask)[1]
-            return dqt + jnp.dot(far_kt_ref[:, at], ds, preferred_element_type=F32)
+
+            def mask():
+                return from_start(t, lo_ref, c * CHUNK - SPAN, key, 0)
+
+            def body(mask, dqt):
+                ds = back_scores(qt, kv_ref[at, HD:], kv_ref[at, :HD], gt, mask)[1]
+                return dqt + jnp.dot(far_kt_ref[:, at], ds, preferred_element_type=F32)
+
+            return with_mask(c * CHUNK - SPAN >= latest_start(t, lo_ref), mask, body, dqt)
 
         def keys(start, size, dqt):
             at = pl.ds(start, size)
-            mask = from_start(t, lo_ref, start, key[:size], 0) & ((key - query)[:size] <= t * TILE - start)
-            w, ds = back_scores(qt, act_ref[at, K], act_ref[at, V], gt, mask)
-            dkv_ref[at, :HD] += jnp.dot(w, g, preferred_element_type=F32)
-            dkv_ref[at, HD:] += jnp.dot(ds, q, preferred_element_type=F32)
-            return dqt + jnp.dot(kt_ref[:, at], ds, preferred_element_type=F32)
+
+            def mask():
+                return from_start(t, lo_ref, start, key[:size], 0) & ((key - query)[:size] <= t * TILE - start)
+
+            def body(mask, dqt):
+                w, ds = back_scores(qt, act_ref[at, K], act_ref[at, V], gt, mask)
+                dkv_ref[at, :HD] += jnp.dot(w, g, preferred_element_type=F32)
+                dkv_ref[at, HD:] += jnp.dot(ds, q, preferred_element_type=F32)
+                return dqt + jnp.dot(kt_ref[:, at], ds, preferred_element_type=F32)
+
+            visible = (start >= latest_start(t, lo_ref)) & (start + size <= t * TILE)
+            return with_mask(visible, mask, body, dqt)
 
         first = lo_ref[2 * t]
         start = jnp.minimum(first + SPAN, SPAN) // CHUNK
@@ -378,11 +414,17 @@
 
         def k_chunk(c, carry):
             at = chunk_at(c)
-            mask = from_start(TILES + t, lo_ref, c * CHUNK, key, 0)
-            w, ds = back_scores(qt, act_ref[at, K], act_ref[at, V], gt, mask)
-            acc_s[at, :HD] += jnp.dot(w, g, preferred_element_type=F32)
-            acc_s[at, HD:] += jnp.dot(ds, q, preferred_element_type=F32)
-            return carry
+
+            def mask():
+                return from_start(TILES + t, lo_ref, c * CHUNK, key, 0)
+
+            def body(mask, carry):
+                w, ds = back_scores(qt, act_ref[at, K], act_ref[at, V], gt, mask)
+                acc_s[at, :HD] += jnp.dot(w, g, preferred_element_type=F32)
+                acc_s[at, HD:] += jnp.dot(ds, q, preferred_element_type=F32)
+                return carry
+
+            return with_mask(c * CHUNK >= latest_start(TILES + t, lo_ref), mask, body, carry)
 
         return lax.fori_loop(lo_ref[2 * (TILES + t)] // CHUNK, CHUNKS, k_chunk, carry)
 

time: 127 us -> 123 us (0.969)
  starting transfers between devices: 45.9 us -> 32 us
  waiting for transfers between devices: 35.9 us -> 43.2 us
  Pallas kernels: 43.8 us -> 47.1 us
    ppermute x2, starting transfers between devices: 16.6 us -> 2.6 us  [between(): return lax.ppermute(x, 'g', [(i, i ^ mask) for i in range(groups)])]
    ppermute x2, waiting for transfers between devices: 3.12 us -> 8.4 us  [backward(): return lax.ppermute(x, 'g', [(i + 1, i) for i in range(groups - 1)])]
    pallas_call x21, Pallas kernels: 43.8 us -> 47.1 us  [call(): pl.pallas_call(kernel, out_shape=[jax.ShapeDtypeStruct(*out) for out in o...]
    ppermute x21, waiting for transfers between devices: 21.8 us -> 23.5 us  [swap(): return lax.ppermute(x, 'h', [(i, i ^ mask) for i in range(HEADS)])]
  transfers between devices with their start and end apart: 27 -> 27, of which waited for: 13 -> 14; matrix products, arithmetic and copies ran while one was open for 0% -> 0% of each run, Pallas kernels for 31% -> 31%
where the time goes in v2:
time: 123 us; the launch traced here: 125 us
  Pallas kernels  47.1 us (38%)
  waiting for transfers between devices  43.2 us (35%)
  starting transfers between devices  32 us (26%)
  local copies, waits for them, and re-layouts  1.34 us (1%)
    pallas_call x21, Pallas kernels, call(): pl.pallas_call(kernel, out_shape=[jax.ShapeDtypeStruct(*out) for out in o...  47.1 us
    ppermute x21, waiting for transfers between devices, swap(): return lax.ppermute(x, 'h', [(i, i ^ mask) for i in range(HEADS)])  23.5 us
    ppermute x21, starting transfers between devices, swap(): return lax.ppermute(x, 'h', [(i, i ^ mask) for i in range(HEADS)])  18.6 us
    ppermute x2, waiting for transfers between devices, between(): return lax.ppermute(x, 'g', [(i, i ^ mask) for i in range(groups)])  8.96 us
    ppermute x2, waiting for transfers between devices, backward(): return lax.ppermute(x, 'g', [(i + 1, i) for i in range(groups - 1)])  8.4 us
    ppermute x2, starting transfers between devices, onward(): return lax.ppermute(x, 'g', [(i, i + 1) for i in range(groups - 1)])  8.08 us
    ppermute x2, starting transfers between devices, backward(): return lax.ppermute(x, 'g', [(i + 1, i) for i in range(groups - 1)])  2.76 us
    ppermute x2, starting transfers between devices, between(): return lax.ppermute(x, 'g', [(i, i ^ mask) for i in range(groups)])  2.6 us
  transfers between devices with their start and end apart: 27, of which 14 were waited for; matrix products, arithmetic and copies ran while one was open for 0% of the time, Pallas kernels for 31%

profile of v2, /device:TPU:0, one launch (start us, length us, event | category | flops | bytes accessed | tf_op | source)
XLA Modules:
  0.0 124.7 jit_solution(16126169165833704663)
XLA Ops:
  1.2 2.6 %collective-permute-start.1 = (bf16[256,1024]{1,0:T(8,128)(2,1)}, bf16[256,1024]{1,0:T(8,128)(2,1)S(1)}, u32[]{:S(2)}, u32[]{:S(2)}) collective-permute-start(bf16[256,1024]{1,0:T(8,128)(2,1)} %refs_9_.1), channel_id=1, source_target_pairs={{0,4},{1,5},{2,6},{3,7},{4,0},{5,1},{6,2},{7,3},{8,12},{9,13},{10,... | collective-permute-start | bytes 1572872 | tf_op jit(solution)/shard_map/ppermute | solution.py:549
  3.8 1.5 %collective-permute-start = (bf16[256,1024]{1,0:T(8,128)(2,1)}, bf16[256,1024]{1,0:T(8,128)(2,1)S(1)}, u32[]{:S(2)}, u32[]{:S(2)}) collective-permute-start(bf16[256,1024]{1,0:T(8,128)(2,1)} %refs_9_.1), channel_id=1, source_target_pairs={{0,2},{1,3},{2,0},{3,1},{4,6},{5,7},{6,4},{7,5},{8,10},{9,11},{10,... | collective-permute-start | bytes 1572872 | tf_op jit(solution)/shard_map/ppermute | solution.py:549
  6.6 2.4 %shard_map.85 = (s32[32]{0:T(128)S(1)}, s32[32]{0:T(128)S(1)}, s32[2]{0:T(128)S(1)}, bf16[1024,512]{1,0:T(8,128)(2,1)S(1)}) custom-call(s32[16]{0:T(128)S(1)} %copy-done.3, s32[16]{0:T(128)S(1)} %copy-done.4, bf16[1024,4096]{1,0:T(8,128)(2,1)} %refs_12_.1), custom_call_target="tpu_custom_call" | custom-call | tf_op jit(solution)/shard_map/pallas_call | solution.py:531
  9.0 1.7 %shard_map.86 = (bf16[2048,1024]{1,0:T(8,128)(2,1)S(1)}, bf16[2048,512]{1,0:T(8,128)(2,1)S(1)}, bf16[2048,512]{1,0:T(8,128)(2,1)S(1)}, bf16[512,256]{1,0:T(8,128)(2,1)S(1)}) custom-call(s32[2]{0:T(128)S(1)} %get-tuple-element.66.at_ref, bf16[256,1024]{1,0:T(8,128)(2,1)S(1)} %copy-done.1, bf16[256,1024]{1,0:T(8,128)(2,1)S(1)} %collective-permute-done.2.refs_1_, ...), custom_call_target="tpu_custom_call" | custom-call | tf_op jit(solution)/shard_map/pallas_call | solution.py:531
  10.7 1.4 %shard_map.87 = (bf16[256,128]{1,0:T(8,128)(2,1)S(1)}, bf16[1024,128]{1,0:T(8,128)(2,1)S(1)}, bf16[512,128]{1,0:T(8,128)(2,1)S(1)}, bf16[512,128]{1,0:T(8,128)(2...) custom-call(s32[2]{0:T(128)S(1)} %get-tuple-element.66.at_ref, bf16[256,1024]{1,0:T(8,128)(2,1)S(1)} %copy-done.2, ...), custom_call_target="tpu_custom_call" | custom-call | tf_op jit(solution)/shard_map/pallas_call | solution.py:531
  12.1 4.4 %collective-permute-done.1.y_ref = bf16[256,1024]{1,0:T(8,128)(2,1)S(1)} collective-permute-done((bf16[256,1024]{1,0:T(8,128)(2,1)}, bf16[256,1024]{1,0:T(8,128)(2,1)S(1)}, u32[]{:S(2)}, u32[]{:S(2)}) %collective-permute-start.1) | collective-permute-done | bytes 524320 | tf_op jit(solution)/shard_map/ppermute | solution.py:549
  16.5 1.5 %collective-permute-done.x_ref = bf16[256,1024]{1,0:T(8,128)(2,1)S(1)} collective-permute-done((bf16[256,1024]{1,0:T(8,128)(2,1)}, bf16[256,1024]{1,0:T(8,128)(2,1)S(1)}, u32[]{:S(2)}, u32[]{:S(2)}) %collective-permute-start) | collective-permute-done | bytes 524320 | tf_op jit(solution)/shard_map/ppermute | solution.py:549
  18.9 1.7 %collective-permute-start.4 = (bf16[128,1024]{1,0:T(8,128)(2,1)S(1)}, bf16[128,1024]{1,0:T(8,128)(2,1)S(1)}, u32[]{:S(2)}, u32[]{:S(2)}) collective-permute-start(bf16[128,1024]{1,0:T(8,128)(2,1)S(1)} %get-tuple-element.72), channel_id=1, source_target_pairs={{0,2},{1,3},{2,0},{3,1},{4,6},{5,7},{6,4},{7,5},{8,10},{9,11},{10,... | collective-permute-start | bytes 786440 | tf_op jit(solution)/shard_map/ppermute | solution.py:549
  20.7 2.6 %shard_map.89 = (bf16[2048,1024]{1,0:T(8,128)(2,1)S(1)}, bf16[2048,512]{1,0:T(8,128)(2,1)S(1)}, bf16[2048,512]{1,0:T(8,128)(2,1)S(1)}, bf16[1536,256]{1,0:T(8,128)(2,1)S(1)}) custom-call(s32[2]{0:T(128)S(1)} %get-tuple-element.66.at_ref, bf16[256,1024]{1,0:T(8,128)(2,1)S(1)} %get-tuple-element.73.refs_0_, ...), custom_call_target="tpu_custom_call", output_to_operand_aliasing={{0}: (7, {}), {1}: (8, {}), {2}: (9, {})} | custom-call | tf_op jit(solution)/shard_map/pallas_call | solution.py:531
  23.3 3.5 %collective-permute-start.9 = (bf16[1536,256]{1,0:T(8,128)(2,1)S(1)}, bf16[1536,256]{1,0:T(8,128)(2,1)S(1)}, u32[]{:S(2)}, u32[]{:S(2)}) collective-permute-start(bf16[1536,256]{1,0:T(8,128)(2,1)S(1)} %get-tuple-element.78.refs_2_), channel_id=1, source_target_pairs={{0,8},{8,16},{16,24},{1,9},{9,17},{17,25},{2,10},{10,18},{18,26},{... | collective-permute-start | bytes 2359304 | tf_op jit(solution)/shard_map/ppermute | solution.py:552
  28.9 1.8 %shard_map.91 = (bf16[2048,1024]{1,0:T(8,128)(2,1)S(1)}, bf16[2048,512]{1,0:T(8,128)(2,1)S(1)}, bf16[2048,512]{1,0:T(8,128)(2,1)S(1)}, bf16[512,256]{1,0:T(8,128)(2,1)S(1)}, bf16[2048,128]{1,0:T(8,128)(2,1)S(1)}) custom-call(s32[2]{0:T(128)S(1)} %get-tuple-element.66.at_ref, ...), custom_call_target="tpu_custom_call", output_to_operand_aliasing={{0}: (6, {}), {1}: (7, {}), {2}: (8, {})} | custom-call | tf_op jit(solution)/shard_map/pallas_call | solution.py:531
  30.7 1.3 %collective-permute-start.19 = (bf16[2048,128]{1,0:T(8,128)(2,1)S(1)}, bf16[2048,128]{1,0:T(8,128)(2,1)S(1)}, u32[]{:S(2)}, u32[]{:S(2)}) collective-permute-start(bf16[2048,128]{1,0:T(8,128)(2,1)S(1)} %get-tuple-element.102), channel_id=1, source_target_pairs={{8,0},{16,8},{24,16},{9,1},{17,9},{25,17},{10,2},{18,10},{26,18},{... | collective-permute-start | bytes 1572872 | tf_op jit(solution)/shard_map/ppermute | solution.py:555
  32.0 1.7 %collective-permute-start.12 = (bf16[512,128]{1,0:T(8,128)(2,1)S(1)}, bf16[512,128]{1,0:T(8,128)(2,1)S(1)}, u32[]{:S(2)}, u32[]{:S(2)}) collective-permute-start(bf16[512,128]{1,0:T(8,128)(2,1)S(1)} %get-tuple-element.97), channel_id=1, source_target_pairs={{0,2},{1,3},{2,0},{3,1},{4,6},{5,7},{6,4},{7,5},{8,10},{9,11},{10,... | collective-permute-start | bytes 393224 | tf_op jit(solution)/shard_map/ppermute | solution.py:549
  33.7 4.5 %collective-permute-start.10 = (bf16[512,256]{1,0:T(8,128)(2,1)S(1)}, bf16[512,256]{1,0:T(8,128)(2,1)S(1)}, u32[]{:S(2)}, u32[]{:S(2)}) collective-permute-start(bf16[512,256]{1,0:T(8,128)(2,1)S(1)} %get-tuple-element.90.refs_3_), channel_id=1, source_target_pairs={{0,8},{8,16},{16,24},{1,9},{9,17},{17,25},{2,10},{10,18},{18,26},{... | collective-permute-start | bytes 786440 | tf_op jit(solution)/shard_map/ppermute | solution.py:552
  38.2 1.6 %collective-permute-start.13 = (bf16[512,128]{1,0:T(8,128)(2,1)S(1)}, bf16[512,128]{1,0:T(8,128)(2,1)S(1)}, u32[]{:S(2)}, u32[]{:S(2)}) collective-permute-start(bf16[512,128]{1,0:T(8,128)(2,1)S(1)} %get-tuple-element.98), channel_id=1, source_target_pairs={{0,4},{1,5},{2,6},{3,7},{4,0},{5,1},{6,2},{7,3},{8,12},{9,13},{10,... | collective-permute-start | bytes 393224 | tf_op jit(solution)/shard_map/ppermute | solution.py:549
  40.2 7.0 %shard_map.92 = (f32[2048,128]{1,0:T(8,128)S(1)}, bf16[128,2048]{1,0:T(8,128)(2,1)S(1)}, bf16[128,2048]{1,0:T(8,128)(2,1)S(1)}, bf16[128,2048]{1,0:T(8,128)(2,1)S(1)}) custom-call(s32[32]{0:T(128)S(1)} %get-tuple-element.67.lo_ref, s32[32]{0:T(128)S(1)} %get-tuple-element.85.nv_ref, bf16[2048,512]{1,0:T(8,128)(2,1)S(1)} %get-tuple-element.84.act_ref, ...), custom_call_target="tpu_custom_call" | custom-call | tf_op jit(solution)/shard_map/pallas_call | solution.py:531
  47.2 2.4 %collective-permute-done.10.kvb_ref = bf16[512,256]{1,0:T(8,128)(2,1)S(1)} collective-permute-done((bf16[512,256]{1,0:T(8,128)(2,1)S(1)}, bf16[512,256]{1,0:T(8,128)(2,1)S(1)}, u32[]{:S(2)}, u32[]{:S(2)}) %collective-permute-start.10) | collective-permute-done | bytes 262176 | tf_op jit(solution)/shard_map/ppermute | solution.py:552
  51.9 1.4 %collective-permute-start.18 = (f32[16,256]{1,0:T(8,128)S(1)}, f32[16,256]{1,0:T(8,128)S(1)}, u32[]{:S(2)}, u32[]{:S(2)}) collective-permute-start(f32[16,256]{1,0:T(8,128)S(1)} %shard_map.95.refs_0_), channel_id=1, source_target_pairs={{0,6},{1,7},{2,4},{3,5},{4,2},{5,3},{6,0},{7,1},{8,14},{9,15},{10,... | collective-permute-start | bytes 49160 | tf_op jit(solution)/shard_map/ppermute | solution.py:549
  53.4 1.5 %collective-permute-start.17 = (f32[16,256]{1,0:T(8,128)S(1)}, f32[16,256]{1,0:T(8,128)S(1)}, u32[]{:S(2)}, u32[]{:S(2)}) collective-permute-start(f32[16,256]{1,0:T(8,128)S(1)} %shard_map.95.refs_0_), channel_id=1, source_target_pairs={{0,4},{1,5},{2,6},{3,7},{4,0},{5,1},{6,2},{7,3},{8,12},{9,13},{10,... | collective-permute-start | bytes 49160 | tf_op jit(solution)/shard_map/ppermute | solution.py:549
  57.1 1.5 %collective-permute-done.16.refs_1_ = f32[16,256]{1,0:T(8,128)S(1)} collective-permute-done((f32[16,256]{1,0:T(8,128)S(1)}, f32[16,256]{1,0:T(8,128)S(1)}, u32[]{:S(2)}, u32[]{:S(2)}) %collective-permute-start.16) | collective-permute-done | bytes 16416 | tf_op jit(solution)/shard_map/ppermute | solution.py:549
  58.6 1.9 %shard_map.96 = (bf16[2048,128]{1,0:T(8,128)(2,1)S(1)}, bf16[128,2048]{1,0:T(8,128)(2,1)S(1)}) custom-call(s32[32]{0:T(128)S(1)} %get-tuple-element.85.nv_ref, s32[2]{0:T(128)S(1)} %get-tuple-element.66.at_ref, bf16[2048,512]{1,0:T(8,128)(2,1)S(1)} %get-tuple-element.84.act_ref, bf16[2048,512]{1,0:T(8,128)(2,1)S(1)} %get-tuple-element.86.slope_ref, ...), custom_call_target="tpu_custom_call" | custom-call | tf_op jit(solution)/shard_map/pallas_call | solution.py:531
  60.5 1.5 %collective-permute-start.20 = (bf16[2048,128]{1,0:T(8,128)(2,1)S(1)}, bf16[2048,128]{1,0:T(8,128)(2,1)S(1)}, u32[]{:S(2)}, u32[]{:S(2)}) collective-permute-start(bf16[2048,128]{1,0:T(8,128)(2,1)S(1)} %get-tuple-element.103.g_ref), channel_id=1, source_target_pairs={{8,0},{16,8},{24,16},{9,1},{17,9},{25,17},{10,2},{18,10},{26,18},{... | collective-permute-start | bytes 1572872 | tf_op jit(solution)/shard_map/ppermute | solution.py:555
  62.0 9.5 %shard_map.97 = (bf16[128,2048]{1,0:T(8,128)(2,1)S(1)}, bf16[2048,128]{1,0:T(8,128)(2,1)S(1)}, f32[2048,256]{1,0:T(8,128)S(1)}) custom-call(s32[32]{0:T(128)S(1)} %get-tuple-element.67.lo_ref, bf16[2048,512]{1,0:T(8,128)(2,1)S(1)} %get-tuple-element.84.act_ref, bf16[128,2048]{1,0:T(8,128)(2,1)S(1)} %get-tuple-element.87.slope_qt_ref, ...), custom_call_target="tpu_custom_call" | custom-call | tf_op jit(solution)/shard_map/pallas_call | solution.py:531
  71.5 8.4 %collective-permute-done.20.g_ref = bf16[2048,128]{1,0:T(8,128)(2,1)S(1)} collective-permute-done((bf16[2048,128]{1,0:T(8,128)(2,1)S(1)}, bf16[2048,128]{1,0:T(8,128)(2,1)S(1)}, u32[]{:S(2)}, u32[]{:S(2)}) %collective-permute-start.20) | collective-permute-done | bytes 524320 | tf_op jit(solution)/shard_map/ppermute | solution.py:555
  79.9 6.3 %shard_map.98 = (bf16[256,512]{1,0:T(8,128)(2,1)S(1)}, bf16[1024,512]{1,0:T(8,128)(2,1)S(1)}, bf16[512,512]{1,0:T(8,128)(2,1)S(1)}, bf16[512,512]{1,0:T(8,128)(2...) custom-call(s32[32]{0:T(128)S(1)} %get-tuple-element.67.lo_ref, s32[2]{0:T(128)S(1)} %get-tuple-element.66.at_ref, ...), custom_call_target="tpu_custom_call" | custom-call | tf_op jit(solution)/shard_map/pallas_call | solution.py:531
  86.3 3.1 %shard_map.103 = (f32[256,1024]{1,0:T(8,128)S(1)}, bf16[256,1024]{1,0:T(8,128)(2,1)S(1)}) custom-call(s32[2]{0:T(128)S(1)} %get-tuple-element.66.at_ref, bf16[128,2048]{1,0:T(8,128)(2,1)S(1)} %get-tuple-element.121.u_cols_ref, bf16[128,2048]{1,0:T(8,128)(2,1)S(1)} %get-tuple-element.122.q_cols_ref, ...), custom_call_target="tpu_custom_call" | custom-call | tf_op jit(solution)/shard_map/pallas_call | solution.py:531
  89.4 2.5 %collective-permute-start.25 = (bf16[256,1024]{1,0:T(8,128)(2,1)S(1)}, bf16[256,1024]{1,0:T(8,128)(2,1)S(1)}, u32[]{:S(2)}, u32[]{:S(2)}) collective-permute-start(bf16[256,1024]{1,0:T(8,128)(2,1)S(1)} %get-tuple-element.125), channel_id=1, source_target_pairs={{0,8},{8,0},{16,24},{24,16},{1,9},{9,1},{17,25},{25,17},{2,10},{10... | collective-permute-start | bytes 1572872 | tf_op jit(solution)/shard_map/ppermute | solution.py:650
  93.4 2.2 %collective-permute-start.24 = (bf16[512,512]{1,0:T(8,128)(2,1)S(1)}, bf16[512,512]{1,0:T(8,128)(2,1)S(1)}, u32[]{:S(2)}, u32[]{:S(2)}) collective-permute-start(bf16[512,512]{1,0:T(8,128)(2,1)S(1)} %get-tuple-element.115), channel_id=1, source_target_pairs={{0,6},{1,7},{2,4},{3,5},{4,2},{5,3},{6,0},{7,1},{8,14},{9,15},{10,... | collective-permute-start | bytes 1572872 | tf_op jit(solution)/shard_map/ppermute | solution.py:549
  95.5 9.0 %collective-permute-done.25.got_ref = bf16[256,1024]{1,0:T(8,128)(2,1)S(1)} collective-permute-done((bf16[256,1024]{1,0:T(8,128)(2,1)S(1)}, bf16[256,1024]{1,0:T(8,128)(2,1)S(1)}, u32[]{:S(2)}, u32[]{:S(2)}) %collective-permute-start.25) | collective-permute-done | bytes 524320 | tf_op jit(solution)/shard_map/ppermute | solution.py:650
  106.8 10.8 %collective-permute-done.23.refs_3_ = bf16[512,512]{1,0:T(8,128)(2,1)S(1)} collective-permute-done((bf16[512,512]{1,0:T(8,128)(2,1)S(1)}, bf16[512,512]{1,0:T(8,128)(2,1)S(1)}, u32[]{:S(2)}, u32[]{:S(2)}) %collective-permute-start.23) | collective-permute-done | bytes 524320 | tf_op jit(solution)/shard_map/ppermute | solution.py:549
  117.6 2.2 %shard_map.100.refs_5_ = f32[256,1024]{1,0:T(8,128)S(1)} custom-call(s32[2]{0:T(128)S(1)} %get-tuple-element.66.at_ref, bf16[256,512]{1,0:T(8,128)(2,1)S(1)} %get-tuple-element.108.refs_0_, bf16[1024,512]{1,0:T(8,128)(2,1)S(1)} %collective-permute-done.21.other_ref.refs_1_, bf16[512,512]{1,0:T(8,128)(2,1)S(1)} %collective-permute-done.22.refs_2_, ...), custom_call_target="tpu_custom_call" | custom-call | tf_op jit(solution)/shard_map/pallas_call | solution.py:531
  119.7 4.1 %shard_map.102 = (bf16[256,1024]{1,0:T(8,128)(2,1)}, bf16[256,1024]{1,0:T(8,128)(2,1)}, f32[8,128]{1,0:T(8,128)S(1)}) custom-call(s32[2]{0:T(128)S(1)} %get-tuple-element.66.at_ref, bf16[256,512]{1,0:T(8,128)(2,1)S(1)} %get-tuple-element.108.refs_0_, bf16[1024,512]{1,0:T(8,128)(2,1)S(1)} %collective-permute-done.21.other_ref.refs_1_, ...), custom_call_target="tpu_custom_call" | custom-call | tf_op jit(solution)/shard_map/pallas_call | solution.py:531
  (58 shorter events, 14.5 us)
Async XLA Ops:
  0.6 8.4 %copy-start.1 = (bf16[256,1024]{1,0:T(8,128)(2,1)S(1)}, bf16[256,1024]{1,0:T(8,128)(2,1)}, u32[]{:S(2)}) copy-start(bf16[256,1024]{1,0:T(8,128)(2,1)} %refs_9_.1) | copy-start | bytes 1572868
  0.6 8.3 %collective-permute-start.2 = (bf16[256,1024]{1,0:T(8,128)(2,1)}, bf16[256,1024]{1,0:T(8,128)(2,1)S(1)}, u32[]{:S(2)}, u32[]{:S(2)}) collective-permute-start(bf16[256,1024]{1,0:T(8,128)(2,1)} %refs_9_.1), channel_id=1, source_target_pairs={{0,1},{1,0},{2,3},{3,2},{4,5},{5,4},{6,7},{7,6},{8,9},{9,8},{10,11... | collective-permute-start | bytes 1572872 | tf_op jit(solution)/shard_map/ppermute | solution.py:549
  1.2 15.3 %collective-permute-start.1 = (bf16[256,1024]{1,0:T(8,128)(2,1)}, bf16[256,1024]{1,0:T(8,128)(2,1)S(1)}, u32[]{:S(2)}, u32[]{:S(2)}) collective-permute-start(bf16[256,1024]{1,0:T(8,128)(2,1)} %refs_9_.1), channel_id=1, source_target_pairs={{0,4},{1,5},{2,6},{3,7},{4,0},{5,1},{6,2},{7,3},{8,12},{9,13},{10,... | collective-permute-start | bytes 1572872 | tf_op jit(solution)/shard_map/ppermute | solution.py:549
  3.8 14.2 %collective-permute-start = (bf16[256,1024]{1,0:T(8,128)(2,1)}, bf16[256,1024]{1,0:T(8,128)(2,1)S(1)}, u32[]{:S(2)}, u32[]{:S(2)}) collective-permute-start(bf16[256,1024]{1,0:T(8,128)(2,1)} %refs_9_.1), channel_id=1, source_target_pairs={{0,2},{1,3},{2,0},{3,1},{4,6},{5,7},{6,4},{7,5},{8,10},{9,11},{10,... | collective-permute-start | bytes 1572872 | tf_op jit(solution)/shard_map/ppermute | solution.py:549
  6.6 4.1 %copy-start.2 = (bf16[256,1024]{1,0:T(8,128)(2,1)S(1)}, bf16[256,1024]{1,0:T(8,128)(2,1)}, u32[]{:S(2)}) copy-start(bf16[256,1024]{1,0:T(8,128)(2,1)} %refs_10_.1) | copy-start | bytes 1572868
  9.0 1.7 %copy-start = (bf16[1024,1024]{1,0:T(8,128)(2,1)S(1)}, bf16[1024,1024]{1,0:T(8,128)(2,1)}, u32[]{:S(2)}) copy-start(bf16[1024,1024]{1,0:T(8,128)(2,1)} %refs_11_.1) | copy-start | bytes 6291460
  18.0 2.6 %collective-permute-start.5 = (bf16[256,1024]{1,0:T(8,128)(2,1)S(1)}, bf16[256,1024]{1,0:T(8,128)(2,1)S(1)}, u32[]{:S(2)}, u32[]{:S(2)}) collective-permute-start(bf16[256,1024]{1,0:T(8,128)(2,1)S(1)} %get-tuple-element.73.refs_0_), channel_id=1, source_target_pairs={{0,1},{1,0},{2,3},{3,2},{4,5},{5,4},{6,7},{7,6},{8,9},{9,8},{10,11... | collective-permute-start | bytes 1572872 | tf_op jit(solution)/shard_map/ppermute | solution.py:549
  18.1 2.6 %collective-permute-start.6 = (bf16[256,1024]{1,0:T(8,128)(2,1)S(1)}, bf16[256,1024]{1,0:T(8,128)(2,1)S(1)}, u32[]{:S(2)}, u32[]{:S(2)}) collective-permute-start(bf16[256,1024]{1,0:T(8,128)(2,1)S(1)} %get-tuple-element.74.refs_2_), channel_id=1, source_target_pairs={{0,1},{1,0},{2,3},{3,2},{4,5},{5,4},{6,7},{7,6},{8,9},{9,8},{10,11... | collective-permute-start | bytes 1572872 | tf_op jit(solution)/shard_map/ppermute | solution.py:549
  18.6 8.3 %collective-permute-start.3 = (bf16[128,1024]{1,0:T(8,128)(2,1)S(1)}, bf16[128,1024]{1,0:T(8,128)(2,1)S(1)}, u32[]{:S(2)}, u32[]{:S(2)}) collective-permute-start(bf16[128,1024]{1,0:T(8,128)(2,1)S(1)} %get-tuple-element.71), channel_id=1, source_target_pairs={{0,4},{1,5},{2,6},{3,7},{4,0},{5,1},{6,2},{7,3},{8,12},{9,13},{10,... | collective-permute-start | bytes 786440 | tf_op jit(solution)/shard_map/ppermute | solution.py:549
  18.9 8.0 %collective-permute-start.4 = (bf16[128,1024]{1,0:T(8,128)(2,1)S(1)}, bf16[128,1024]{1,0:T(8,128)(2,1)S(1)}, u32[]{:S(2)}, u32[]{:S(2)}) collective-permute-start(bf16[128,1024]{1,0:T(8,128)(2,1)S(1)} %get-tuple-element.72), channel_id=1, source_target_pairs={{0,2},{1,3},{2,0},{3,1},{4,6},{5,7},{6,4},{7,5},{8,10},{9,11},{10,... | collective-permute-start | bytes 786440 | tf_op jit(solution)/shard_map/ppermute | solution.py:549
  23.3 26.2 %collective-permute-start.9 = (bf16[1536,256]{1,0:T(8,128)(2,1)S(1)}, bf16[1536,256]{1,0:T(8,128)(2,1)S(1)}, u32[]{:S(2)}, u32[]{:S(2)}) collective-permute-start(bf16[1536,256]{1,0:T(8,128)(2,1)S(1)} %get-tuple-element.78.refs_2_), channel_id=1, source_target_pairs={{0,8},{8,16},{16,24},{1,9},{9,17},{17,25},{2,10},{10,18},{18,26},{... | collective-permute-start | bytes 2359304 | tf_op jit(solution)/shard_map/ppermute | solution.py:552
  26.9 1.6 %collective-permute-start.7 = (bf16[128,1024]{1,0:T(8,128)(2,1)S(1)}, bf16[128,1024]{1,0:T(8,128)(2,1)S(1)}, u32[]{:S(2)}, u32[]{:S(2)}) collective-permute-start(bf16[128,1024]{1,0:T(8,128)(2,1)S(1)} %get-tuple-element.79.refs_0_), channel_id=1, source_target_pairs={{0,1},{1,0},{2,3},{3,2},{4,5},{5,4},{6,7},{7,6},{8,9},{9,8},{10,11... | collective-permute-start | bytes 786440 | tf_op jit(solution)/shard_map/ppermute | solution.py:549
  27.0 1.9 %collective-permute-start.8 = (bf16[128,1024]{1,0:T(8,128)(2,1)S(1)}, bf16[128,1024]{1,0:T(8,128)(2,1)S(1)}, u32[]{:S(2)}, u32[]{:S(2)}) collective-permute-start(bf16[128,1024]{1,0:T(8,128)(2,1)S(1)} %get-tuple-element.80.refs_1_), channel_id=1, source_target_pairs={{0,1},{1,0},{2,3},{3,2},{4,5},{5,4},{6,7},{7,6},{8,9},{9,8},{10,11... | collective-permute-start | bytes 786440 | tf_op jit(solution)/shard_map/ppermute | solution.py:549
  27.5 4.5 %collective-permute-start.11 = (bf16[1024,128]{1,0:T(8,128)(2,1)S(1)}, bf16[1024,128]{1,0:T(8,128)(2,1)S(1)}, u32[]{:S(2)}, u32[]{:S(2)}) collective-permute-start(bf16[1024,128]{1,0:T(8,128)(2,1)S(1)} %get-tuple-element.93), channel_id=1, source_target_pairs={{0,1},{1,0},{2,3},{3,2},{4,5},{5,4},{6,7},{7,6},{8,9},{9,8},{10,11... | collective-permute-start | bytes 786440 | tf_op jit(solution)/shard_map/ppermute | solution.py:549
  30.7 24.8 %collective-permute-start.19 = (bf16[2048,128]{1,0:T(8,128)(2,1)S(1)}, bf16[2048,128]{1,0:T(8,128)(2,1)S(1)}, u32[]{:S(2)}, u32[]{:S(2)}) collective-permute-start(bf16[2048,128]{1,0:T(8,128)(2,1)S(1)} %get-tuple-element.102), channel_id=1, source_target_pairs={{8,0},{16,8},{24,16},{9,1},{17,9},{25,17},{10,2},{18,10},{26,18},{... | collective-permute-start | bytes 1572872 | tf_op jit(solution)/shard_map/ppermute | solution.py:555
  32.0 7.8 %collective-permute-start.12 = (bf16[512,128]{1,0:T(8,128)(2,1)S(1)}, bf16[512,128]{1,0:T(8,128)(2,1)S(1)}, u32[]{:S(2)}, u32[]{:S(2)}) collective-permute-start(bf16[512,128]{1,0:T(8,128)(2,1)S(1)} %get-tuple-element.97), channel_id=1, source_target_pairs={{0,2},{1,3},{2,0},{3,1},{4,6},{5,7},{6,4},{7,5},{8,10},{9,11},{10,... | collective-permute-start | bytes 393224 | tf_op jit(solution)/shard_map/ppermute | solution.py:549
  33.7 15.9 %collective-permute-start.10 = (bf16[512,256]{1,0:T(8,128)(2,1)S(1)}, bf16[512,256]{1,0:T(8,128)(2,1)S(1)}, u32[]{:S(2)}, u32[]{:S(2)}) collective-permute-start(bf16[512,256]{1,0:T(8,128)(2,1)S(1)} %get-tuple-element.90.refs_3_), channel_id=1, source_target_pairs={{0,8},{8,16},{16,24},{1,9},{9,17},{17,25},{2,10},{10,18},{18,26},{... | collective-permute-start | bytes 786440 | tf_op jit(solution)/shard_map/ppermute | solution.py:552
  38.2 8.9 %collective-permute-start.13 = (bf16[512,128]{1,0:T(8,128)(2,1)S(1)}, bf16[512,128]{1,0:T(8,128)(2,1)S(1)}, u32[]{:S(2)}, u32[]{:S(2)}) collective-permute-start(bf16[512,128]{1,0:T(8,128)(2,1)S(1)} %get-tuple-element.98), channel_id=1, source_target_pairs={{0,4},{1,5},{2,6},{3,7},{4,0},{5,1},{6,2},{7,3},{8,12},{9,13},{10,... | collective-permute-start | bytes 393224 | tf_op jit(solution)/shard_map/ppermute | solution.py:549
  39.8 7.3 %collective-permute-start.14 = (bf16[512,128]{1,0:T(8,128)(2,1)S(1)}, bf16[512,128]{1,0:T(8,128)(2,1)S(1)}, u32[]{:S(2)}, u32[]{:S(2)}) collective-permute-start(bf16[512,128]{1,0:T(8,128)(2,1)S(1)} %get-tuple-element.99), channel_id=1, source_target_pairs={{0,6},{1,7},{2,4},{3,5},{4,2},{5,3},{6,0},{7,1},{8,14},{9,15},{10,... | collective-permute-start | bytes 393224 | tf_op jit(solution)/shard_map/ppermute | solution.py:549
  50.7 1.2 collective-permute-start.15
  51.9 4.6 %collective-permute-start.18 = (f32[16,256]{1,0:T(8,128)S(1)}, f32[16,256]{1,0:T(8,128)S(1)}, u32[]{:S(2)}, u32[]{:S(2)}) collective-permute-start(f32[16,256]{1,0:T(8,128)S(1)} %shard_map.95.refs_0_), channel_id=1, source_target_pairs={{0,6},{1,7},{2,4},{3,5},{4,2},{5,3},{6,0},{7,1},{8,14},{9,15},{10,... | collective-permute-start | bytes 49160 | tf_op jit(solution)/shard_map/ppermute | solution.py:549
  53.4 3.7 %collective-permute-start.17 = (f32[16,256]{1,0:T(8,128)S(1)}, f32[16,256]{1,0:T(8,128)S(1)}, u32[]{:S(2)}, u32[]{:S(2)}) collective-permute-start(f32[16,256]{1,0:T(8,128)S(1)} %shard_map.95.refs_0_), channel_id=1, source_target_pairs={{0,4},{1,5},{2,6},{3,7},{4,0},{5,1},{6,2},{7,3},{8,12},{9,13},{10,... | collective-permute-start | bytes 49160 | tf_op jit(solution)/shard_map/ppermute | solution.py:549
  54.9 3.7 %collective-permute-start.16 = (f32[16,256]{1,0:T(8,128)S(1)}, f32[16,256]{1,0:T(8,128)S(1)}, u32[]{:S(2)}, u32[]{:S(2)}) collective-permute-start(f32[16,256]{1,0:T(8,128)S(1)} %shard_map.95.refs_0_), channel_id=1, source_target_pairs={{0,2},{1,3},{2,0},{3,1},{4,6},{5,7},{6,4},{7,5},{8,10},{9,11},{10,... | collective-permute-start | bytes 49160 | tf_op jit(solution)/shard_map/ppermute | solution.py:549
  60.5 19.4 %collective-permute-start.20 = (bf16[2048,128]{1,0:T(8,128)(2,1)S(1)}, bf16[2048,128]{1,0:T(8,128)(2,1)S(1)}, u32[]{:S(2)}, u32[]{:S(2)}) collective-permute-start(bf16[2048,128]{1,0:T(8,128)(2,1)S(1)} %get-tuple-element.103.g_ref), channel_id=1, source_target_pairs={{8,0},{16,8},{24,16},{9,1},{17,9},{25,17},{10,2},{18,10},{26,18},{... | collective-permute-start | bytes 1572872 | tf_op jit(solution)/shard_map/ppermute | solution.py:555
  79.9 24.8 %slice-start = ((s8[8388608]{0:T(1024)(128)(4,1)}), s8[4194304]{0:T(1024)(128)(4,1)S(1)}, s32[]{:S(2)}) async-start(s8[8388608]{0:T(1024)(128)(4,1)} %bitcast), calls=%async_computation | async-start | bytes 8388608
  86.2 5.7 %collective-permute-start.21 = (bf16[1024,512]{1,0:T(8,128)(2,1)S(1)}, bf16[1024,512]{1,0:T(8,128)(2,1)S(1)}, u32[]{:S(2)}, u32[]{:S(2)}) collective-permute-start(bf16[1024,512]{1,0:T(8,128)(2,1)S(1)} %get-tuple-element.109), channel_id=1, source_target_pairs={{0,1},{1,0},{2,3},{3,2},{4,5},{5,4},{6,7},{7,6},{8,9},{9,8},{10,11... | collective-permute-start | bytes 3145736 | tf_op jit(solution)/shard_map/ppermute | solution.py:549
  86.3 18.4 %slice-start.1 = ((s8[8388608]{0:T(1024)(128)(4,1)}), s8[4194304]{0:T(1024)(128)(4,1)S(1)}, s32[]{:S(2)}) async-start(s8[8388608]{0:T(1024)(128)(4,1)} %bitcast), calls=%async_computation.1 | async-start | bytes 8388608
  89.4 15.1 %collective-permute-start.25 = (bf16[256,1024]{1,0:T(8,128)(2,1)S(1)}, bf16[256,1024]{1,0:T(8,128)(2,1)S(1)}, u32[]{:S(2)}, u32[]{:S(2)}) collective-permute-start(bf16[256,1024]{1,0:T(8,128)(2,1)S(1)} %get-tuple-element.125), channel_id=1, source_target_pairs={{0,8},{8,0},{16,24},{24,16},{1,9},{9,1},{17,25},{25,17},{2,10},{10... | collective-permute-start | bytes 1572872 | tf_op jit(solution)/shard_map/ppermute | solution.py:650
  92.0 14.8 %collective-permute-start.22 = (bf16[512,512]{1,0:T(8,128)(2,1)S(1)}, bf16[512,512]{1,0:T(8,128)(2,1)S(1)}, u32[]{:S(2)}, u32[]{:S(2)}) collective-permute-start(bf16[512,512]{1,0:T(8,128)(2,1)S(1)} %get-tuple-element.113), channel_id=1, source_target_pairs={{0,2},{1,3},{2,0},{3,1},{4,6},{5,7},{6,4},{7,5},{8,10},{9,11},{10,... | collective-permute-start | bytes 1572872 | tf_op jit(solution)/shard_map/ppermute | solution.py:549
  92.6 25.0 %collective-permute-start.23 = (bf16[512,512]{1,0:T(8,128)(2,1)S(1)}, bf16[512,512]{1,0:T(8,128)(2,1)S(1)}, u32[]{:S(2)}, u32[]{:S(2)}) collective-permute-start(bf16[512,512]{1,0:T(8,128)(2,1)S(1)} %get-tuple-element.114), channel_id=1, source_target_pairs={{0,4},{1,5},{2,6},{3,7},{4,0},{5,1},{6,2},{7,3},{8,12},{9,13},{10,... | collective-permute-start | bytes 1572872 | tf_op jit(solution)/shard_map/ppermute | solution.py:549
  93.4 26.4 %collective-permute-start.24 = (bf16[512,512]{1,0:T(8,128)(2,1)S(1)}, bf16[512,512]{1,0:T(8,128)(2,1)S(1)}, u32[]{:S(2)}, u32[]{:S(2)}) collective-permute-start(bf16[512,512]{1,0:T(8,128)(2,1)S(1)} %get-tuple-element.115), channel_id=1, source_target_pairs={{0,6},{1,7},{2,4},{3,5},{4,2},{5,3},{6,0},{7,1},{8,14},{9,15},{10,... | collective-permute-start | bytes 1572872 | tf_op jit(solution)/shard_map/ppermute | solution.py:549
  104.6 19.2 %collective-permute-start.26 = (bf16[128,1024]{1,0:T(8,128)(2,1)S(1)}, bf16[128,1024]{1,0:T(8,128)(2,1)S(1)}, u32[]{:S(2)}, u32[]{:S(2)}) collective-permute-start(bf16[128,1024]{1,0:T(8,128)(2,1)S(1)} %get-tuple-element.127), channel_id=1, source_target_pairs={{0,16},{8,24},{16,0},{24,8},{1,17},{9,25},{17,1},{25,9},{2,18},{10... | collective-permute-start | bytes 786440 | tf_op jit(solution)/shard_map/ppermute | solution.py:650
  (2 other events, 1.3 us)
